TPU v7x, 32 devices: a whole 2x2x4 slice. The times are simulated.
32 devices in a mesh: blk: 4 (over y, x), cells: 8 (over z, core).
Axes of the slice: x: 2, y: 2, z: 4, core: 2. Of those that a mesh axis runs over, the one named last changes fastest.
Arguments:
- tokens: bfloat16 [24, 1536, 512], P('cells', 'blk'), may hold values from -6 to 6
- known_flags: int32 [24, 1536], P('cells'), may hold values 0 or 1
- w_query: bfloat16 [512, 512], replicated, may hold values from -0.25 to 0.25
- b_query: bfloat16 [512], replicated, may hold values from -2 to 2
- w_key: bfloat16 [512, 512], replicated, may hold values from -0.25 to 0.25
- w_value: bfloat16 [512, 512], replicated, may hold values from -0.25 to 0.25
- b_value: bfloat16 [512], replicated, may hold values from -2 to 2
- w_out: bfloat16 [512, 512], replicated, may hold values from -6 to 6
- b_out: bfloat16 [512], replicated, may hold values from -2 to 2
- gain_one: bfloat16 [512], replicated, may hold values from 0.5 to 1.5
- shift_one: bfloat16 [512], replicated, may hold values from -2 to 2
- w_up: bfloat16 [512, 512], replicated, may hold values from -0.25 to 0.25
- b_up: bfloat16 [512], replicated, may hold values from -2 to 2
- w_down: bfloat16 [512, 512], replicated, may hold values from -0.25 to 0.25
- b_down: bfloat16 [512], replicated, may hold values from -2 to 2
- gain_two: bfloat16 [512], replicated, may hold values from 0.5 to 1.5
- shift_two: bfloat16 [512], replicated, may hold values from -2 to 2
- cotangent: bfloat16 [24, 1536, 512], P('cells', 'blk'), may hold values from -6 to 6
Outputs:
- layer_out: bfloat16 [24, 1536, 512], P('cells', 'blk')
- grad_tokens: float32 [24, 1536, 512], P('cells', 'blk')
- grad_w_query: float32 [512, 512], replicated
- grad_b_query: float32 [512], replicated
- grad_w_key: float32 [512, 512], replicated
- grad_w_value: float32 [512, 512], replicated
- grad_b_value: float32 [512], replicated
- grad_w_out: float32 [512, 512], replicated
- grad_b_out: float32 [512], replicated
- grad_gain_one: float32 [512], replicated
- grad_shift_one: float32 [512], replicated
- grad_w_up: float32 [512, 512], replicated
- grad_b_up: float32 [512], replicated
- grad_w_down: float32 [512, 512], replicated
- grad_b_down: float32 [512], replicated
- grad_gain_two: float32 [512], replicated
- grad_shift_two: float32 [512], replicated
All inputs are finite; a program needn't handle non-finite values. No bound on the sum of `known_flags` on one device may be relied on, other than what follows from the above.
Results may differ from a plain program's by a relative error of at most 0.015.
Values may be sent and summed in bfloat16 or wider, within the bound.
No kernel may reach another device: no remote copies, remote signals or barrier semaphores. Data moves between devices by JAX's collectives and lax.ppermute only.
A program may use at most 256 MiB of HBM per device.

v0:
```python
import functools
import math

import jax
import jax.numpy as jnp
from jax import lax
from jax.experimental import pallas as pl
from jax.experimental.pallas import tpu as pltpu
from jax.sharding import PartitionSpec as P

HEADS = 8
EPSILON = 1e-05
LOG2E = math.log2(math.e)
NONE = -1e30
NN = (((1,), (0,)), ((), ()))
NT = (((1,), (1,)), ((), ()))
TN = (((0,), (0,)), ((), ()))
f32 = jnp.float32
bf16 = jnp.bfloat16
SMALL_BYTES = 6 * 1024 * 1024
INPUTS_BYTES = 20 * 1024 * 1024
FORWARD_BYTES = 20 * 1024 * 1024
MIDDLE_BYTES = 20 * 1024 * 1024
BACKWARD_BYTES = 40 * 1024 * 1024
UNROLL = 8


def dot(a, b, dims=NN):
    return lax.dot_general(a, b, dims, preferred_element_type=f32)


def sizes_of(length):
    return [length * 13 // 24 // 64 * 64, length]


def by_size(count, sizes, run):
    low = 0
    for at, size in enumerate(sizes):
        fits = count <= size
        if at:
            fits = fits & (count > low)
        pl.when(fits)(functools.partial(run, size))
        low = size


def pad_heads(padded, whole):
    heads, double, _ = padded.shape
    size = double // 2
    blank = jnp.zeros((size, whole.shape[1]), whole.dtype)
    for h in range(heads):
        part = whole[h * size : (h + 1) * size, :]
        padded[h] = jnp.concatenate([part, blank] if h % 2 == 0 else [blank, part], 0)


def over_heads(run, heads, rows, common):
    if common:

        def step(i, carry):
            for t in range(UNROLL):
                run(UNROLL * i + t, 0, rows)
            return carry

        lax.fori_loop(0, heads // UNROLL, step, 0)
    else:
        wide = 128
        chunks = rows // wide

        def step(i, carry):
            run(i // chunks, pl.multiple_of(i % chunks * wide, wide), wide)
            return carry

        lax.fori_loop(0, heads * chunks, step, 0)


def prepare_kernel(here_ref, near_ref, far_ref, tokens_ref, cot_ref, place_ref, *sent):
    x, y, core = here_ref[0], here_ref[1], here_ref[2]
    count = tokens_ref.shape[1] // 2
    sent, cots = sent[:4], sent[4:]
    for at, ref in enumerate(sent):
        rows = pl.ds(pl.multiple_of((y ^ (at % 2)) * count, count), count)
        ref[...] = tokens_ref[2, rows, :]
        cots[at][0] = cot_ref[x ^ (at // 2), rows, :]
        if at < 2:
            cots[at][1] = cot_ref[2, rows, :]
    length = near_ref.shape[1]
    part = length // 8
    flags = jnp.where(core == y, near_ref[...], far_ref[...]).astype(f32)
    flags = jnp.concatenate([jnp.where(x == 1, flags[1:2], flags[0:1]), flags[2:3]], 0)
    pieces = {}
    for at in range(8):
        pieces[at // 4, at // 2 % 2, at % 2] = flags[:, at * part : (at + 1) * part]
    for bit, axis in ((core, 2), (x, 1)):
        turn = lambda k, axis=axis: tuple(1 - v if n == axis else v for n, v in enumerate(k))
        pieces = {k: jnp.where(bit == 1, pieces[turn(k)], v) for k, v in pieces.items()}
    ordered = []
    for side in range(2):
        for i in range(2):
            for j in range(2):
                swapped = core != side
                ordered.append(jnp.where(swapped, pieces[1 - j, i, side], pieces[j, i, side]))
    flags = jnp.concatenate(ordered, 1)
    width = 128
    rows = lax.broadcasted_iota(jnp.int32, (width, width), 0)
    lower = (rows <= lax.broadcasted_iota(jnp.int32, (width, width), 1)).astype(f32).astype(bf16)
    tiles = jnp.concatenate([flags[:, at : at + width] for at in range(0, length, width)], 0)
    inside = dot(tiles.astype(bf16), lower)
    ahead = jnp.full((2, 1), -1.0, f32)
    placed = []
    for at in range(length // width):
        tile = inside[2 * at : 2 * at + 2, :]
        placed.append(tile + ahead)
        ahead = ahead + tile[:, width - 1 :]
    place_ref[...] = jnp.where(flags > 0, jnp.concatenate(placed, 1), -1.0)


def prepare(here, near, far, tokens, cotangent):
    _, rows, model = tokens.shape
    vmem = pl.BlockSpec(memory_space=pltpu.VMEM)
    sent = [jax.ShapeDtypeStruct((rows // 2, model), bf16)] * 4
    sent += [jax.ShapeDtypeStruct((n, rows // 2, model), bf16) for n in (2, 2, 1, 1)]
    return pl.pallas_call(
        prepare_kernel,
        out_shape=[jax.ShapeDtypeStruct((2, near.shape[1]), f32), *sent],
        in_specs=[pl.BlockSpec(memory_space=pltpu.SMEM)] + [vmem] * 4,
        out_specs=[vmem] * 9,
        compiler_params=pltpu.CompilerParams(vmem_limit_bytes=SMALL_BYTES),
        name="prepare",
    )(here, near, far, tokens, cotangent)


def count_of(place):
    return (jnp.max(place) + 1.0).astype(jnp.int32)


def column(row, lanes):
    return jnp.broadcast_to(row, (lanes, row.shape[1])).T[:, 0:1]


def join_kernel(layout, after, *refs):
    outs = refs[len(refs) - len(layout) :]
    for out_ref, pieces in zip(outs, layout):
        count = out_ref.shape[0] // len(pieces)
        for at, (source, place) in enumerate(pieces):
            piece = refs[source][...] if place is None else refs[source][place]
            out_ref[at * count : (at + 1) * count, :] = piece


def join(pieces, layout, after=()):
    count, model = pieces[0].shape[-2:]
    vmem = pl.BlockSpec(memory_space=pltpu.VMEM)
    anywhere = pl.BlockSpec(memory_space=pl.ANY)
    return pl.pallas_call(
        functools.partial(join_kernel, layout, len(after)),
        out_shape=[jax.ShapeDtypeStruct((count * len(p), model), bf16) for p in layout],
        in_specs=[vmem] * len(pieces) + [anywhere] * len(after),
        out_specs=[vmem] * len(layout),
        compiler_params=pltpu.CompilerParams(vmem_limit_bytes=SMALL_BYTES),
        name="join",
    )(*pieces, *after)


def forward_kernel(
    sizes,
    cell,
    place_ref,
    own_ref,
    other_ref,
    wqT_ref,
    wkT_ref,
    wk_ref,
    wvT_ref,
    vec_ref,
    mix_ref,
    lse_ref,
    self_ref,
    q_hbm,
    ko_hbm,
    vo_hbm,
    packed_hbm,
    keys_hbm,
    q_ref,
    ko_ref,
    vo_ref,
    packed_ref,
    keys_ref,
    v_s,
    q_s,
    sems,
):
    heads, size, rows = q_ref.shape
    scale = size ** (-0.5) * LOG2E
    place = place_ref[cell : cell + 1, :]
    count = count_of(place)
    half = own_ref.shape[0]
    length = 2 * half
    b_value = column(vec_ref[7:8, :], 8)
    x_own = own_ref[0:rows, :]
    q = (dot(wqT_ref[...], x_own, NT) + column(vec_ref[8:9, :], 8)).astype(bf16)
    ko = dot(wkT_ref[...], x_own, NT).astype(bf16)
    vo = (dot(wvT_ref[...], x_own, NT) + b_value).astype(bf16)
    q_ref[...] = q.reshape(heads, size, rows)
    ko_ref[...] = ko.reshape(heads, size, rows)
    vo_ref[...] = vo.reshape(heads, size, rows)
    held = ((q_ref, q_hbm), (ko_ref, ko_hbm), (vo_ref, vo_hbm))
    saves = [pltpu.make_async_copy(*pair, sems.at[n]) for n, pair in enumerate(held)]
    for save in saves:
        save.start()
    own_score = (q.astype(f32) * ko.astype(f32)).reshape(heads, size, rows).sum(1, keepdims=True)
    self_ref[...] = jnp.where(place[None, :, 0:rows] < 0, own_score * scale, NONE)
    pad_heads(q_s, q)

    def run(n):
        spot = lax.broadcasted_iota(jnp.int32, (n, half), 0).astype(f32)
        pick_own = (spot == place[:, 0:half]).astype(f32).astype(bf16)
        pick_other = (spot == place[:, half:]).astype(f32).astype(bf16)
        packed = (dot(pick_own, own_ref[...]) + dot(pick_other, other_ref[...])).astype(bf16)
        packed_ref[0:n, :] = packed
        keys = dot(packed, wk_ref[...]).astype(bf16)
        keys_ref[0:n, :] = keys
        first = pl.ds(0, n)
        held = ((packed_ref, packed_hbm), (keys_ref, keys_hbm))
        late = [
            pltpu.make_async_copy(near.at[first], far.at[first], sems.at[3 + at])
            for at, (near, far) in enumerate(held)
        ]
        for save in late:
            save.start()
        v_s[:, :, 0:n] = (
            (dot(wvT_ref[...], packed, NT) + b_value).astype(bf16).reshape(heads, size, n)
        )

        def head(h, at, wide):
            pair = pl.ds(pl.multiple_of(h // 2 * 2 * size, 2 * size), 2 * size)
            raw = dot(keys_ref[0:n, pair], q_s[h, :, pl.ds(at, wide)])
            seen = lax.broadcasted_iota(jnp.int32, raw.shape, 0) < count
            scores = jnp.where(seen, raw * scale, NONE)
            own = self_ref[h, :, pl.ds(at, wide)]
            top = jnp.maximum(jnp.max(scores, axis=0, keepdims=True), own)
            weights = jnp.exp2(scores - top)
            own_weight = jnp.exp2(own - top)
            total = jnp.sum(weights, axis=0, keepdims=True) + own_weight
            mixed = dot(v_s[h, :, 0:n], weights.astype(bf16))
            mixed = mixed + own_weight * vo_ref[h, :, pl.ds(at, wide)].astype(f32)
            mix_ref[h, :, pl.ds(at, wide)] = (mixed / total).astype(bf16)
            lse_ref[h, :, pl.ds(at, wide)] = top + jnp.log(total) * LOG2E

        over_heads(head, heads, rows, n < length)
        for save in late:
            save.wait()

    by_size(count, sizes, run)
    for save in saves:
        save.wait()


def attention_forward(cell, place, own, other, weights, rows):
    held = [pltpu.with_memory_space_constraint(w, pltpu.HBM) for w in weights]
    weights = held if cell else (*weights[:-1], held[-1])
    half, model = own.shape
    length = 2 * half
    size = model // HEADS
    vmem = pl.BlockSpec(memory_space=pltpu.VMEM)
    by_head = pltpu.VMEM((HEADS, size, rows), bf16)
    by_key = pltpu.VMEM((length, model), bf16)
    head_rows = jax.ShapeDtypeStruct((HEADS, size, rows), bf16)
    row_stat = jax.ShapeDtypeStruct((HEADS, 1, rows), f32)
    return pl.pallas_call(
        functools.partial(forward_kernel, sizes_of(length), cell),
        out_shape=(
            head_rows,
            row_stat,
            row_stat,
            *[pltpu.HBM(head_rows.shape, bf16)] * 3,
            *[pltpu.HBM((length, model), bf16)] * 2,
        ),
        in_specs=[vmem] * (3 + len(weights)),
        out_specs=(vmem,) * 3 + (pl.BlockSpec(memory_space=pltpu.HBM),) * 5,
        scratch_shapes=[
            by_head,
            by_head,
            by_head,
            by_key,
            by_key,
            pltpu.VMEM((HEADS, size, length), bf16),
            pltpu.VMEM((HEADS, 2 * size, rows), bf16),
            pltpu.SemaphoreType.DMA((5,)),
        ],
        compiler_params=pltpu.CompilerParams(vmem_limit_bytes=FORWARD_BYTES),
        cost_estimate=pl.CostEstimate(
            flops=16 * rows * length * model, bytes_accessed=8 << 20, transcendentals=0
        ),
        name="attention_forward",
    )(place, own, other, *weights)


def split_halves(here_ref, mine_ref, other_ref, whole_ref, small):
    count = whole_ref.shape[0] // 2
    core = here_ref[2]
    for ref, side in ((mine_ref, core), (other_ref, 1 - core)):
        ref[0:count, :] = whole_ref[pl.ds(pl.multiple_of(side * count, count), count), :]
        ref[count:, :] = small.astype(bf16)


def middle_kernel(
    here_ref,
    mix_a_ref,
    x_a_ref,
    mix_b_ref,
    x_b_ref,
    cot_0_ref,
    cot_1_ref,
    cot_2_ref,
    cot_3_ref,
    w_out_ref,
    w_up_ref,
    w_down_ref,
    vec_ref,
    *rest,
):
    outs_a, outs_b, (mine_ref, other_ref, mix_ref, x_ref, cot_ref, w_acc, v_acc, w_low) = (
        rest[:4],
        rest[4:8],
        rest[8:],
    )
    step = pl.program_id(0)
    last = pl.num_programs(0) - 1
    model = x_ref.shape[1]

    @pl.when(step == 0)
    def _():
        w_acc[...] = jnp.zeros_like(w_acc)
        v_acc[...] = jnp.zeros_like(v_acc)

    part = cot_ref.shape[0] // 2
    for at, pair in enumerate(((cot_0_ref, cot_1_ref), (cot_2_ref, cot_3_ref))):

        @pl.when(step == at)
        def _():
            mix_ref[...] = mix_a_ref[...]
            x_ref[...] = x_a_ref[...]
            cot_ref[0:part, :] = pair[0][0]
            cot_ref[part:, :] = pair[1][0]

    @pl.when(step == last)
    def _():
        mix_ref[...] = mix_b_ref[...]
        x_ref[...] = x_b_ref[...]
        cot_ref[0:part, :] = cot_0_ref[1]
        cot_ref[part:, :] = cot_1_ref[1]

    b_out, gain_one, shift_one, b_up, b_down, gain_two, shift_two = (
        vec_ref[i : i + 1, :] for i in range(7)
    )

    def mean(v):
        return jnp.mean(v, axis=-1, keepdims=True)

    def rows(v):
        return jnp.sum(v, axis=0, keepdims=True)

    attn_in = mix_ref[...]
    h1 = x_ref[...].astype(f32) + dot(attn_in, w_out_ref[...], TN) + b_out
    c1 = h1 - mean(h1)
    inv1 = lax.rsqrt(mean(c1 * c1) + EPSILON)
    n1 = c1 * inv1
    x1 = n1 * gain_one + shift_one
    x1_low = x1.astype(bf16)
    up = dot(x1_low, w_up_ref[...]) + b_up
    cdf = 0.5 + 0.5 * lax.erf(up * (0.5**0.5))
    slope = cdf + up * (jnp.exp(-0.5 * up * up) * (1.0 / math.sqrt(2.0 * math.pi)))
    act = (up * cdf).astype(bf16)
    h2 = x1 + dot(act, w_down_ref[...]) + b_down
    c2 = h2 - mean(h2)
    inv2 = lax.rsqrt(mean(c2 * c2) + EPSILON)
    n2 = c2 * inv2
    out = (n2 * gain_two + shift_two).astype(bf16)
    cot = cot_ref[...].astype(f32)
    g_gain_two = rows(cot * n2)
    g_shift_two = rows(cot)
    gn2 = cot * gain_two
    gh2 = inv2 * (gn2 - mean(gn2) - n2 * mean(gn2 * n2))
    g_down = gh2.astype(bf16)
    w_acc[2 * model :, :] += dot(act, g_down, TN)
    g_b_down = rows(g_down.astype(f32))
    g_up = (slope * dot(g_down, w_down_ref[...], NT)).astype(bf16)
    w_acc[model : 2 * model, :] += dot(x1_low, g_up, TN)
    g_b_up = rows(g_up.astype(f32))
    gx1 = gh2 + dot(g_up, w_up_ref[...], NT)
    g_gain_one = rows(gx1 * n1)
    g_shift_one = rows(gx1)
    gn1 = gx1 * gain_one
    gh1 = inv1 * (gn1 - mean(gn1) - n1 * mean(gn1 * n1))
    g_attn = gh1.astype(bf16)
    w_acc[0:model, :] += dot(attn_in, g_attn)
    g_b_out = rows(g_attn.astype(f32))
    g_mix = dot(w_out_ref[...], g_attn, NT).astype(bf16)
    size = model // HEADS
    delta = (g_mix.astype(f32) * attn_in.astype(f32)).reshape(HEADS, size, -1).sum(1, keepdims=True)
    results = (out, gh1, g_mix.reshape(HEADS, size, -1), delta)
    sums = (g_b_out, g_gain_one, g_shift_one, g_b_up, g_b_down, g_gain_two, g_shift_two)
    for at, term in enumerate(sums):
        v_acc[at : at + 1, :] += term

    @pl.when(step < last)
    def _():
        for ref, value in zip(outs_a, results):
            ref[...] = value

    @pl.when(step == last)
    def _():
        for ref, value in zip(outs_b, results):
            ref[...] = value
        w_low[...] = w_acc[...].astype(bf16)
        split_halves(here_ref, mine_ref, other_ref, w_low, v_acc[...])


def middle(here, mix, x, cot, weights, vectors):
    _, part, model = cot[0].shape
    block = 2 * part
    size = model // HEADS
    steps = 2
    whole = lambda shape: pl.BlockSpec(shape, lambda i: (0,) * len(shape))
    places = (lambda i: jnp.minimum(i, steps - 1), lambda i: 0)
    by_row = [pl.BlockSpec((block, model), lambda i, at=at: (at(i), 0)) for at in places]
    by_column = [pl.BlockSpec((model, block), lambda i, at=at: (0, at(i))) for at in places]
    by_head = [pl.BlockSpec((HEADS, size, block), lambda i, at=at: (0, 0, at(i))) for at in places]
    stats = [pl.BlockSpec((HEADS, 1, block), lambda i, at=at: (0, 0, at(i))) for at in places]
    square = whole((model, model))
    half_shape = (3 * model // 2 + 16, model)
    inputs, in_specs, out_shape, out_specs = [], [], [], []
    for k in range(2):
        rows = mix[k].shape[1]
        inputs += [mix[k], x[k]]
        in_specs += [by_column[k], by_row[k]]
        out_shape += [
            jax.ShapeDtypeStruct((rows, model), bf16),
            jax.ShapeDtypeStruct((rows, model), f32),
            jax.ShapeDtypeStruct((HEADS, size, rows), bf16),
            jax.ShapeDtypeStruct((HEADS, 1, rows), f32),
        ]
        out_specs += [by_row[k], by_row[k], by_head[k], stats[k]]
    return pl.pallas_call(
        middle_kernel,
        grid=(steps + 1,),
        out_shape=(
            *out_shape,
            jax.ShapeDtypeStruct(half_shape, bf16),
            jax.ShapeDtypeStruct(half_shape, bf16),
        ),
        in_specs=[
            pl.BlockSpec(memory_space=pltpu.SMEM),
            *in_specs,
            *[whole(piece.shape) for piece in cot],
            square,
            square,
            square,
            whole(vectors.shape),
        ],
        out_specs=(*out_specs, whole(half_shape), whole(half_shape)),
        scratch_shapes=[
            pltpu.VMEM((model, block), bf16),
            pltpu.VMEM((block, model), bf16),
            pltpu.VMEM((block, model), bf16),
            pltpu.VMEM((3 * model, model), f32),
            pltpu.VMEM((16, model), f32),
            pltpu.VMEM((3 * model, model), bf16),
        ],
        compiler_params=pltpu.CompilerParams(
            vmem_limit_bytes=MIDDLE_BYTES, dimension_semantics=("arbitrary",)
        ),
        cost_estimate=pl.CostEstimate(
            flops=36 * (steps + 1) * block * model * model,
            bytes_accessed=8 << 20,
            transcendentals=0,
        ),
        name="middle",
    )(here, *inputs, *cot, *weights, vectors)


def backward_kernel(
    sizes,
    has_before,
    after,
    cell,
    here_ref,
    place_ref,
    own_ref,
    wkT_ref,
    wv_ref,
    vec_ref,
    q_hbm,
    ko_hbm,
    vo_hbm,
    packed_hbm,
    keys_hbm,
    lse_ref,
    self_ref,
    gmix_ref,
    delta_ref,
    *rest,
):
    if has_before:
        before_w_ref, before_v_ref, *rest = rest
    rest = rest[after:]
    gk_hbm, gv_hbm, gq_hbm, gko_hbm, gvo_hbm, first_ref, second_ref, *rest = rest
    q_ref, ko_ref, vo_ref, packed_ref, keys_ref, gk_ref, gv_ref, gq_s, gko_s, gvo_s, *rest = rest
    kT_s, v_s, gk_s, gv_s, w_acc, v_acc, q_s, gm_s, w_low, sems = rest
    heads, size, rows = q_ref.shape
    model = heads * size
    length = packed_ref.shape[0]
    held = ((q_hbm, q_ref), (ko_hbm, ko_ref), (vo_hbm, vo_ref))
    loads = [pltpu.make_async_copy(*pair, sems.at[n]) for n, pair in enumerate(held)]
    for load in loads:
        load.start()
    plain = size ** (-0.5)
    scale = plain * LOG2E
    place = place_ref[cell : cell + 1, :]
    count = count_of(place)
    pad_heads(gm_s, gmix_ref[...].reshape(model, rows))

    def run(n):
        first = pl.ds(0, n)
        held = ((packed_hbm, packed_ref), (keys_hbm, keys_ref))
        late = [
            pltpu.make_async_copy(far.at[first], near.at[first], sems.at[3 + at])
            for at, (far, near) in enumerate(held)
        ]
        for load in late:
            load.start()
        for load in loads:
            load.wait()
        pad_heads(q_s, q_ref[...].reshape(model, rows))
        for load in late:
            load.wait()
        packed = packed_ref[0:n, :]
        kT_s[:, :, 0:n] = dot(wkT_ref[...], packed, NT).astype(bf16).reshape(heads, size, n)
        values = (dot(packed, wv_ref[...]) + vec_ref[7:8, :]).astype(bf16)
        v_s[0:n, :] = values

        def head(h, at, wide):
            here = pl.ds(at, wide)
            pair = pl.ds(pl.multiple_of(h // 2 * 2 * size, 2 * size), 2 * size)
            k_pair = keys_ref[0:n, pair]
            v_pair = v_s[0:n, pair]
            q_full = q_s[h, :, here]
            gm_full = gm_s[h, :, here]
            lse = lse_ref[h, :, here]
            delta = delta_ref[h, :, here]
            raw = dot(k_pair, q_full)
            seen = lax.broadcasted_iota(jnp.int32, raw.shape, 0) < count
            weights = jnp.where(seen, jnp.exp2(raw * scale - lse), 0.0)
            g_weights = dot(v_pair, gm_full)
            g_raw = ((plain * weights) * (g_weights - delta)).astype(bf16)
            gv_s[0:n, pair] += dot(weights.astype(bf16), gm_full, NT)
            gk_s[0:n, pair] += dot(g_raw, q_full, NT)
            gq = dot(kT_s[h, :, 0:n], g_raw)
            own_weight = jnp.exp2(self_ref[h, :, here] - lse)
            ko = ko_ref[h, :, here].astype(f32)
            vo = vo_ref[h, :, here].astype(f32)
            gm = gmix_ref[h, :, here].astype(f32)
            g_own = jnp.sum(gm * vo, axis=0, keepdims=True)
            g_own_raw = (plain * own_weight * (g_own - delta)).astype(bf16).astype(f32)
            gq_s[h, :, here] = (gq + g_own_raw * ko).astype(bf16)
            gko_s[h, :, here] = (g_own_raw * q_ref[h, :, here].astype(f32)).astype(bf16)
            gvo_s[h, :, here] = (own_weight * gm).astype(bf16)

        gk_s[0:n, :] = jnp.zeros((n, model), f32)
        gv_s[0:n, :] = jnp.zeros((n, model), f32)
        over_heads(head, heads, rows, n < length)
        gk = gk_s[0:n, :].astype(bf16)
        gv = gv_s[0:n, :].astype(bf16)
        gk_ref[0:n, :] = gk
        gv_ref[0:n, :] = gv
        held = ((gk_ref, gk_hbm), (gv_ref, gv_hbm))
        saves = [
            pltpu.make_async_copy(near.at[first], far.at[first], sems.at[3 + at])
            for at, (near, far) in enumerate(held)
        ]
        for save in saves:
            save.start()
        w_acc[model : 2 * model, :] = dot(gk, packed, TN)
        w_acc[2 * model :, :] = dot(gv, packed, TN)
        v_acc[1:2, :] = jnp.sum(gv.astype(f32), axis=0, keepdims=True)
        for save in saves:
            save.wait()

    by_size(count, sizes, run)
    held = ((gq_s, gq_hbm), (gko_s, gko_hbm), (gvo_s, gvo_hbm))
    saves = [pltpu.make_async_copy(*pair, sems.at[n]) for n, pair in enumerate(held)]
    for save in saves:
        save.start()
    gq = gq_s[...].reshape(model, rows)
    gko = gko_s[...].reshape(model, rows)
    gvo = gvo_s[...].reshape(model, rows)
    x_own = own_ref[0:rows, :]
    ones = jnp.ones((8, rows), bf16)
    w_q = dot(gq, x_own)
    w_k = w_acc[model : 2 * model, :] + dot(gko, x_own)
    w_v = w_acc[2 * model :, :] + dot(gvo, x_own)
    v_q = dot(ones, gq, NT)[0:1, :]
    v_v = v_acc[1:2, :] + dot(ones, gvo, NT)[0:1, :]
    if has_before:
        w_q = w_q + before_w_ref[0:model, :]
        w_k = w_k + before_w_ref[model : 2 * model, :]
        w_v = w_v + before_w_ref[2 * model :, :]
        v_q = v_q + before_v_ref[0:1, :]
        v_v = v_v + before_v_ref[1:2, :]
    if has_before:
        for at, total in enumerate((w_q, w_k, w_v)):
            w_low[at * model : (at + 1) * model, :] = total.T.astype(bf16)
        blank = jnp.zeros((8, model), f32)
        small = jnp.concatenate([blank, v_q, v_v, blank[2:]], 0)
        split_halves(here_ref, first_ref, second_ref, w_low, small)
    else:
        for at, total in enumerate((w_q, w_k, w_v)):
            first_ref[at * model : (at + 1) * model, :] = total
        second_ref[0:1, :] = v_q
        second_ref[1:2, :] = v_v
    for save in saves:
        save.wait()


def attention_backward(cell, here, place, own, weights, saved, stats, before, after, rows):
    half, model = own.shape
    length = 2 * half
    size = model // HEADS
    vmem = pl.BlockSpec(memory_space=pltpu.VMEM)
    before = before or ()
    inputs = (here, place, own, *weights, *saved, *stats, *before, *after)
    hbm = pl.BlockSpec(memory_space=pltpu.HBM)
    anywhere = pl.BlockSpec(memory_space=pl.ANY)
    per_key = pltpu.VMEM((length, model), bf16)
    key_sum = pltpu.VMEM((length, model), f32)
    per_head = pltpu.VMEM((HEADS, size, rows), bf16)
    padded = pltpu.VMEM((HEADS, 2 * size, rows), bf16)
    by_key = pltpu.HBM((length, model), bf16)
    by_head = pltpu.HBM((HEADS, size, rows), bf16)
    if not before:
        sums = [
            jax.ShapeDtypeStruct((3 * model, model), f32),
            jax.ShapeDtypeStruct((8, model), f32),
        ]
    else:
        sums = [jax.ShapeDtypeStruct((3 * model // 2 + 16, model), bf16)] * 2
    return pl.pallas_call(
        functools.partial(backward_kernel, sizes_of(length), bool(before), len(after), cell),
        out_shape=(by_key, by_key, by_head, by_head, by_head, *sums),
        in_specs=[
            pl.BlockSpec(memory_space=pltpu.SMEM),
            *[vmem] * (2 + len(weights)),
            *[hbm] * len(saved),
            *[vmem] * (len(stats) + len(before)),
            *[anywhere] * len(after),
        ],
        out_specs=(hbm,) * 5 + (vmem,) * 2,
        scratch_shapes=[
            per_head,
            per_head,
            per_head,
            per_key,
            per_key,
            per_key,
            per_key,
            per_head,
            per_head,
            per_head,
            pltpu.VMEM((HEADS, size, length), bf16),
            per_key,
            key_sum,
            key_sum,
            pltpu.VMEM((3 * model, model), f32),
            pltpu.VMEM((8, model), f32),
            padded,
            padded,
            pltpu.VMEM((3 * model, model), bf16),
            pltpu.SemaphoreType.DMA((5,)),
        ],
        compiler_params=pltpu.CompilerParams(vmem_limit_bytes=BACKWARD_BYTES),
        cost_estimate=pl.CostEstimate(
            flops=30 * rows * length * model, bytes_accessed=16 << 20, transcendentals=0
        ),
        name="attention_backward",
    )(*inputs)


def inputs_kernel(
    sizes,
    cell,
    after,
    place_ref,
    gk_hbm,
    gv_hbm,
    gq_hbm,
    gko_hbm,
    gvo_hbm,
    wqT_ref,
    wkT_ref,
    wvT_ref,
    gh1_ref,
    *rest,
):
    kept_ref, sent_ref, gk_ref, gv_ref, gq_ref, gko_ref, gvo_ref, full_s, sems = rest[after:]
    held = ((gq_hbm, gq_ref), (gko_hbm, gko_ref), (gvo_hbm, gvo_ref))
    loads = [pltpu.make_async_copy(*pair, sems.at[n]) for n, pair in enumerate(held)]
    heads, size, rows = gq_ref.shape
    length, model = gk_ref.shape
    half = length // 2
    place = place_ref[cell : cell + 1, :]

    def run(n):
        first = pl.ds(0, n)
        late = [
            pltpu.make_async_copy(far.at[first], near.at[first], sems.at[3 + at])
            for at, (far, near) in enumerate(((gk_hbm, gk_ref), (gv_hbm, gv_ref)))
        ]
        for load in late + loads:
            load.start()
        for load in late:
            load.wait()
        g_packed = dot(gk_ref[0:n, :], wkT_ref[...]) + dot(gv_ref[0:n, :], wvT_ref[...])
        spot = lax.broadcasted_iota(jnp.int32, (length, n), 1).astype(f32)
        spread = (spot == column(place, 8)).astype(f32).astype(bf16)
        full_s[...] = dot(spread, g_packed.astype(bf16))

    by_size(count_of(place), sizes, run)
    for load in loads:
        load.wait()
    whole = lambda ref: ref[...].reshape(model, rows)
    mine = dot(whole(gq_ref), wqT_ref[...], TN) + dot(whole(gko_ref), wkT_ref[...], TN)
    mine = mine + dot(whole(gvo_ref), wvT_ref[...], TN)
    kept_ref[0:rows, :] = full_s[0:rows, :] + mine + gh1_ref[...]
    if rows < half:
        kept_ref[rows:, :] = full_s[rows:half, :]
    sent_ref[...] = full_s[half:, :].astype(bf16)


def input_gradients(cell, place, grads, weights, gh1, after):
    length, model = grads[0].shape
    rows = gh1.shape[0]
    vmem = pl.BlockSpec(memory_space=pltpu.VMEM)
    hbm = pl.BlockSpec(memory_space=pltpu.HBM)
    per_key = pltpu.VMEM((length, model), bf16)
    per_head = pltpu.VMEM(grads[2].shape, bf16)
    grads = [pltpu.with_memory_space_constraint(array, pltpu.HBM) for array in grads]
    return pl.pallas_call(
        functools.partial(inputs_kernel, sizes_of(length), cell, len(after)),
        out_shape=(
            jax.ShapeDtypeStruct((length // 2, model), f32),
            jax.ShapeDtypeStruct((length // 2, model), bf16),
        ),
        in_specs=[vmem]
        + [hbm] * 5
        + [vmem] * 4
        + [pl.BlockSpec(memory_space=pl.ANY)] * len(after),
        out_specs=(vmem,) * 2,
        scratch_shapes=[
            per_key,
            per_key,
            per_head,
            per_head,
            per_head,
            pltpu.VMEM((length, model), f32),
            pltpu.SemaphoreType.DMA((5,)),
        ],
        compiler_params=pltpu.CompilerParams(vmem_limit_bytes=INPUTS_BYTES),
        cost_estimate=pl.CostEstimate(
            flops=4 * length * length * model, bytes_accessed=8 << 20, transcendentals=0
        ),
        name="input_gradients",
    )(place, *grads, *weights, gh1, *after)


def exchange(piece, axis, partner):
    count = lax.axis_size(axis)
    return lax.ppermute(piece, axis, [(i, i ^ partner) for i in range(count)])


def radices_of(count):
    radices = []
    while count > 1:
        radix = 4 if count % 4 == 0 else 2
        radices.append(radix)
        count //= radix
    return radices


def reduce_plan():
    plan = [("cells", 2, 1)]
    for axis, stride in (("blk", 1), ("cells", 2)):
        for radix in radices_of(lax.axis_size(axis) // stride):
            plan.append((axis, radix, stride))
            stride *= radix
    return plan


def send_step(step, big, small):
    axis, radix, stride = step
    digit = (lax.axis_index(axis) // stride) % radix
    parts, rows, model = big.shape
    count = rows // radix
    arrived = []
    for other in range(1, radix):
        piece = lax.dynamic_slice_in_dim(big, (digit ^ other) * count, count, 1)
        sent = jnp.concatenate([piece.reshape(parts * count, model), small], 0)
        arrived.append(exchange(sent, axis, other * stride))
    return arrived


def sum_step(step, big, small, arrived):
    axis, radix, stride = step
    digit = (lax.axis_index(axis) // stride) % radix
    parts, rows, model = big.shape
    count = rows // radix
    big = lax.dynamic_slice_in_dim(big, digit * count, count, 1).astype(f32)
    small = small.astype(f32)
    for got in arrived:
        big = big + got[: parts * count].reshape(parts, count, model).astype(f32)
        small = small + got[parts * count :].astype(f32)
    return big.astype(bf16), small.astype(bf16)


def reduce_step(step, big, small):
    return sum_step(step, big, small, send_step(step, big, small))


def core_step(mine, other):
    total = mine.astype(f32) + exchange(other, "cells", 1).astype(f32)
    total = total.astype(bf16)
    count = total.shape[0] - 16
    return total[None, :count], total[count:]


def share_step(step, big):
    axis, radix, stride = step
    return [big] + [exchange(big, axis, other * stride) for other in range(1, radix)]


def gather_step(step, parts):
    axis, radix, stride = step
    digit = (lax.axis_index(axis) // stride) % radix
    ordered = []
    for place in range(radix):
        chosen = parts[place]
        for d in range(1, radix):
            chosen = jnp.where(digit == d, parts[place ^ d], chosen)
        ordered.append(chosen)
    return jnp.concatenate(ordered, 1)


def finish_kernel(here_ref, near_ref, far_ref, *rest):
    outs, (whole_s, sems) = rest[:-2], rest[-2:]
    core = here_ref[2]
    parts, count, model = near_ref.shape
    size = outs[0].shape[0]
    saves = []
    for part in range(parts):
        for ref, side in ((near_ref, core), (far_ref, 1 - core)):
            rows = pl.ds(pl.multiple_of(side * count, count), count)
            whole_s[part, rows, :] = ref[part].astype(f32)
        for at in range(2 * count // size):
            out = part * (2 * count // size) + at
            save = pltpu.make_async_copy(
                whole_s.at[part, pl.ds(at * size, size)], outs[out], sems.at[out]
            )
            save.start()
            saves.append(save)
    for save in saves:
        save.wait()


def finish(here, near, far):
    parts, count, model = near.shape
    number = parts * 2 * count // model
    vmem = pl.BlockSpec(memory_space=pltpu.VMEM)
    return pl.pallas_call(
        finish_kernel,
        out_shape=[pltpu.HBM((model, model), f32)] * number,
        in_specs=[pl.BlockSpec(memory_space=pltpu.SMEM), vmem, vmem],
        out_specs=[pl.BlockSpec(memory_space=pltpu.HBM)] * number,
        scratch_shapes=[
            pltpu.VMEM((parts, 2 * count, model), f32),
            pltpu.SemaphoreType.DMA((number,)),
        ],
        compiler_params=pltpu.CompilerParams(vmem_limit_bytes=INPUTS_BYTES),
        name="finish",
    )(here, near, far)


def swap(parts, flag):
    first, second = parts
    return jnp.where(flag == 1, second, first), jnp.where(flag == 1, first, second)


def body(
    tokens,
    known_flags,
    w_query,
    b_query,
    w_key,
    w_value,
    b_value,
    w_out,
    b_out,
    gain_one,
    shift_one,
    w_up,
    b_up,
    w_down,
    b_down,
    gain_two,
    shift_two,
    cotangent,
):
    cells, rows, model = tokens.shape
    blocks = lax.axis_size("blk")
    others = lax.axis_size("cells")
    part = rows // 2
    half = 2 * rows
    length = 2 * half
    block = lax.axis_index("blk")
    core = lax.axis_index("cells") % 2
    x, y = block % 2, block // 2
    axes = ("blk", "cells")

    def route(i, j):
        pairs = []
        for b in range(blocks):
            for c in range(others):
                there = 2 * (c % 2) + ((b % 2) ^ i)
                pairs.append((b * others + c, there * others + c - c % 2 + ((b // 2) ^ j)))
        return pairs

    def route_back(i, j):
        return [(there, here) for here, there in route(i, j)]

    both = ((0, 0), (0, 1), (1, 0), (1, 1))

    def near_rows(source, j):
        return lax.dynamic_slice_in_dim(source, (y ^ j) * part, part, 1)

    def cell_of(rows_sent, i):
        return lax.dynamic_slice_in_dim(rows_sent, x ^ i, 1, 0)

    turned = (w_query.T, w_key.T, w_value.T)
    vectors = [b_out, gain_one, shift_one, b_up, b_down, gain_two, shift_two, b_value, b_query]
    vectors = jnp.concatenate([jnp.stack(vectors).astype(f32), jnp.zeros((7, model), f32)], 0)
    first = {}
    for i, j in both:
        first[i, j] = lax.ppermute(cell_of(near_rows(tokens, j), i)[0], axes, route(i, j))
    here = jnp.stack([x, y, core]).astype(jnp.int32)
    place, *payloads = prepare(
        here, known_flags, exchange(known_flags, "cells", 1), tokens, cotangent
    )
    rest = {
        ij: lax.ppermute(sent, axes, route(*ij)) for ij, sent in zip(both, payloads[:4])
    }
    cot = [lax.ppermute(sent, axes, route(*ij)) for ij, sent in zip(both, payloads[4:])]
    wqT, wkT, wvT = turned
    pieces = [first[ij] for ij in both]
    own = list(join(pieces, [[(n, None) for n in range(4)]], (place, *turned, vectors)))
    other = [exchange(own[0], "cells", 1)]
    work = (half, rows)

    def attend(k):
        return attention_forward(
            k, place, own[k], other[k], (wqT, wkT, w_key, wvT, vectors), work[k]
        )

    forward = [attend(0)]
    mix = forward[0][0]
    own += join([rest[ij] for ij in both], [[(n, None) for n in range(4)]], (mix,))
    other.append(exchange(own[1], "cells", 1))
    forward.append(attend(1))
    mids = middle(
        here,
        [mix.reshape(model, half), forward[1][0].reshape(model, rows)],
        own,
        cot,
        (w_out, w_up, w_down),
        vectors,
    )
    mids, halves = (mids[:4], mids[4:8]), mids[8:]
    plan = reduce_plan()
    early, early_small = core_step(*halves)

    out_back = {}
    for i, j in both:
        pieces = [mids[0][0][(2 * i + j) * part : (2 * i + j + 1) * part]]
        if i == 0:
            pieces.append(mids[1][0][j * part : (j + 1) * part])
        out_back[i, j] = lax.ppermute(jnp.stack(pieces), axes, route_back(i, j))

    def rejoin(from_i):
        return jnp.concatenate(swap(from_i, y), 0)

    near, far = (rejoin((out_back[i, 0][0], out_back[i, 1][0])) for i in range(2))
    layer_out = jnp.stack([*swap((near, far), x), rejoin((out_back[0, 0][1], out_back[0, 1][1]))])

    def attend_back(k, before, after):
        mix, lse, own_score, *saved = forward[k]
        out, gh1, g_mix, delta = mids[k]
        return attention_backward(
            k,
            here,
            place,
            own[k],
            (wkT, w_value, vectors),
            saved,
            (lse, own_score, g_mix, delta),
            before,
            after,
            work[k],
        )

    def keep(k, grads, after):
        return input_gradients(k, place, grads, (wqT, wkT, wvT), mids[k][1], after)

    def whole_rows(mine, sent):
        return (mine + exchange(sent, "cells", 1).astype(f32)).astype(bf16)

    def give_back(kept):
        back = []
        for n, (i, j) in enumerate(both):
            sent = jnp.stack([rows[n * part : (n + 1) * part] for rows in kept])
            back.append(lax.ppermute(sent, axes, route_back(i, j)))
        return back

    *grads_a, first_sum, second_sum = attend_back(0, None, ())
    *grads_b, mine, other_half = attend_back(1, (first_sum, second_sum), (early, layer_out))
    early, early_small = reduce_step(plan[1], early, early_small)
    mine, other_half, early, early_small = lax.optimization_barrier(
        (mine, other_half, early, early_small)
    )
    late, late_small = core_step(mine, other_half)
    kept = keep(0, grads_a, (late,))
    late, late_small = reduce_step(plan[1], late, late_small)
    late, late_small, kept = lax.optimization_barrier((late, late_small, kept))
    kept_a = whole_rows(*kept)
    kept = keep(1, grads_b, (late,))
    big = jnp.concatenate([early, late], 0)
    small = (early_small.astype(f32) + late_small.astype(f32)).astype(bf16)
    for at, step in enumerate(plan[2:]):
        arrived = send_step(step, big, small)
        if at == 0:
            arrived, kept = lax.optimization_barrier((arrived, kept))
        big, small = sum_step(step, big, small, arrived)
    back = give_back([kept_a, whole_rows(*kept)])
    for step in reversed(plan[2:]):
        parts = share_step(step, big)
        if step is plan[2]:
            parts, back = lax.optimization_barrier((parts, back))
        big = gather_step(step, parts)
    big = gather_step(plan[1], share_step(plan[1], big))

    near, far, near_last, far_last = (
        rejoin((back[2 * i][k], back[2 * i + 1][k])).astype(f32) for k in range(2) for i in range(2)
    )
    grad_tokens = jnp.stack([*swap((near, far), x), near_last + far_last])
    big, small, grad_tokens = lax.optimization_barrier((big, small, grad_tokens))
    g_out, g_up, g_down, g_query, g_key, g_value = finish(here, big, exchange(big, "cells", 1))
    small = small.astype(f32)
    g_b_out, g_gain_one, g_shift_one, g_b_up, g_b_down, g_gain_two, g_shift_two = (
        small[n] for n in range(7)
    )
    return (
        layer_out,
        grad_tokens,
        g_query,
        small[8],
        g_key,
        g_value,
        small[9],
        g_out,
        g_b_out,
        g_gain_one,
        g_shift_one,
        g_up,
        g_b_up,
        g_down,
        g_b_down,
        g_gain_two,
        g_shift_two,
    )


def solution(mesh):
    rows = P("cells", "blk", None)
    return jax.shard_map(
        body,
        mesh=mesh,
        in_specs=(rows, P("cells", None)) + (P(),) * 15 + (rows,),
        out_specs=(rows, rows) + (P(),) * 15,
        check_vma=False,
    )
```

profile of v0, /device:TPU:0, one launch (start us, length us, event | category | flops | bytes accessed | tf_op | source)
XLA Modules:
  0.0 198.2 jit_solution(6949949158843619057)
XLA Ops:
  1.3 2.2 %dynamic-slice_bitcast_fusion = (bf16[192,512]{1,0:T(8,128)(2,1)}, bf16[192,512]{1,0:T(8,128)(2,1)}, bf16[192,512]{1,0:T(8,128)(2,1)}, bf16[192,512]{1,0:T(8,128)(2,1)}) fusion(bf16[3,384,512]{2,1,0:T(8,128)(2,1)} %tokens_ref.1, s32[]{:T(128)S(6)} %select_n.349, s32[]{:T(128)S(6)} %select_n.347, s32[]{:T(128)S(6)} %select_n.343, s32[]{:T(128)S(6)} %select_n.345), kind=kLoop, calls=%fused_computation.58 | loop fusion | bytes 1572880 | tf_op jit(solution)/shard_map/squeeze | solution.py:949
  5.1 3.2 %collective-permute-start.2 = (bf16[192,512]{1,0:T(8,128)(2,1)}, bf16[192,512]{1,0:T(8,128)(2,1)}, u32[]{:S(2)}, u32[]{:S(2)}) collective-permute-start(bf16[192,512]{1,0:T(8,128)(2,1)} %get-tuple-element.187), channel_id=1, source_target_pairs={{0,1},{1,17},{2,3},{3,19},{4,5},{5,21},{6,7},{7,23},{8,9},{9,25},{... | collective-permute-start | bytes 589832 | tf_op jit(solution)/shard_map/ppermute | solution.py:949
  16.4 3.2 %collective-permute-done.4.refs_3_ = bf16[192,512]{1,0:T(8,128)(2,1)} collective-permute-done((bf16[192,512]{1,0:T(8,128)(2,1)}, bf16[192,512]{1,0:T(8,128)(2,1)}, u32[]{:S(2)}, u32[]{:S(2)}) %collective-permute-start.4) | collective-permute-done | bytes 196640 | tf_op jit(solution)/shard_map/ppermute | solution.py:949
  21.6 1.7 collective-permute-start.7
  23.3 1.9 collective-permute-start.8
  26.2 12.9 %attention_forward.2 = (bf16[8,64,768]{2,1,0:T(8,128)(2,1)S(1)}, f32[8,1,768]{2,1,0:T(1,128)S(1)}, f32[8,1,768]{2,1,0:T(1,128)S(1)}, bf16[8,64,768]{2,1,0:T(8,12...) custom-call(f32[2,1536]{1,0:T(2,128)S(1)} %get-tuple-element.100.ref, ...), custom_call_target="tpu_custom_call" | custom-call | flops 9663676416 | bytes 8388608 | tf_op jit(solution)/shard_map/attention_forward/pallas_call | solution.py:267
  41.1 2.0 %collective-permute-start.12 = (bf16[2,192,512]{2,1,0:T(8,128)(2,1)S(1)}, bf16[2,192,512]{2,1,0:T(8,128)(2,1)S(1)}, u32[]{:S(2)}, u32[]{:S(2)}) collective-permute-start(bf16[2,192,512]{2,1,0:T(8,128)(2,1)S(1)} %copy-done.26), channel_id=1, source_target_pairs={{0,1},{1,17},{2,3},{3,19},{4,5},{5,21},{6,7},{7,23},{8,9},{9,25},{... | collective-permute-start | bytes 1179656 | tf_op jit(solution)/shard_map/ppermute | solution.py:957
  43.0 1.7 collective-permute-start.13
  45.7 10.5 %attention_forward.3 = (bf16[8,64,384]{2,1,0:T(8,128)(2,1)S(1)}, f32[8,1,384]{2,1,0:T(1,128)S(1)}, f32[8,1,384]{2,1,0:T(1,128)S(1)}, bf16[8,64,384]{2,1,0:T(8,12...) custom-call(f32[2,1536]{1,0:T(2,128)S(1)} %copy-done.19, ...), custom_call_target="tpu_custom_call" | custom-call | flops 4831838208 | bytes 8388608 | tf_op jit(solution)/shard_map/attention_forward/pallas_call | solution.py:267
  56.2 2.2 %collective-permute-done.12.cot_1_ref = bf16[2,192,512]{2,1,0:T(8,128)(2,1)S(1)} collective-permute-done((bf16[2,192,512]{2,1,0:T(8,128)(2,1)S(1)}, bf16[2,192,512]{2,1,0:T(8,128)(2,1)S(1)}, u32[]{:S(2)}, u32[]{:S(2)}) %collective-permute-start.12) | collective-permute-done | bytes 393248 | tf_op jit(solution)/shard_map/ppermute | solution.py:957
  58.5 13.8 %middle.1 = (bf16[768,512]{1,0:T(8,128)(2,1)S(1)}, f32[768,512]{1,0:T(8,128)S(1)}, bf16[8,64,768]{2,1,0:T(8,128)(2,1)S(1)}, f32[8,1,768]{2,1,0:T(1,128)S(1)}, bf...) custom-call(s32[3]{0:T(128)S(1)} %copy-done.21, ...), custom_call_target="tpu_custom_call" | custom-call | flops 10871635968 | bytes 8388608 | tf_op jit(solution)/shard_map/middle/pallas_call | solution.py:442
  76.9 18.5 %attention_backward.2 = (bf16[1536,512]{1,0:T(8,128)(2,1)}, bf16[1536,512]{1,0:T(8,128)(2,1)}, bf16[8,64,768]{2,1,0:T(8,128)(2,1)}, bf16[8,64,768]{2,1,0:T(8,128...) custom-call(s32[3]{0:T(128)S(1)} %copy-done.21, f32[2,1536]{1,0:T(2,128)S(1)} %copy-done.19, ...), custom_call_target="tpu_custom_call" | custom-call | flops 18119393280 | bytes 16777216 | tf_op jit(solution)/shard_map/attention_backward/pallas_call | solution.py:645
  96.4 1.7 collective-permute-start.20
  100.0 13.6 %attention_backward.3 = (bf16[1536,512]{1,0:T(8,128)(2,1)}, bf16[1536,512]{1,0:T(8,128)(2,1)}, bf16[8,64,384]{2,1,0:T(8,128)(2,1)}, bf16[8,64,384]{2,1,0:T(8,128...) custom-call(s32[3]{0:T(128)S(1)} %copy-done.21, ...), custom_call_target="tpu_custom_call" | custom-call | flops 9059696640 | bytes 16777216 | tf_op jit(solution)/shard_map/attention_backward/pallas_call | solution.py:645
  114.5 2.3 %collective-permute-done.23 = bf16[784,512]{1,0:T(8,128)(2,1)} collective-permute-done((bf16[784,512]{1,0:T(8,128)(2,1)}, bf16[784,512]{1,0:T(8,128)(2,1)}, u32[]{:S(2)}, u32[]{:S(2)}) %collective-permute-start.23) | collective-permute-done | bytes 802848 | tf_op jit(solution)/shard_map/ppermute | solution.py:775
  118.4 1.8 collective-permute-start.24
  121.9 6.0 %input_gradients.2 = (f32[768,512]{1,0:T(8,128)S(1)}, bf16[768,512]{1,0:T(8,128)(2,1)S(1)}) custom-call(f32[2,1536]{1,0:T(2,128)S(1)} %copy-done.19, bf16[1536,512]{1,0:T(8,128)(2,1)} %get-tuple-element.140.gk_hbm, bf16[1536,512]{1,0:T(8,128)(2,1)} %get-tuple-element.141.gv_hbm, bf16[8,64,768]{2,1,0:T(8,128)(2,1)} %get-tuple-element.142.gq_hbm, ...), custom_call_target="tpu_custom_call" | custom-call | flops 4831838208 | bytes 8388608 | tf_op jit(solution)/shard_map/input_gradients/pallas_call | solution.py:745
  128.0 3.9 %collective-permute-done.25 = bf16[208,512]{1,0:T(8,128)(2,1)S(1)} collective-permute-done((bf16[208,512]{1,0:T(8,128)(2,1)S(1)}, bf16[208,512]{1,0:T(8,128)(2,1)S(1)}, u32[]{:S(2)}, u32[]{:S(2)}) %collective-permute-start.25) | collective-permute-done | bytes 213024 | tf_op jit(solution)/shard_map/ppermute | solution.py:775
  132.3 1.6 collective-permute-start.27
  133.9 2.6 %collective-permute-start.28 = (bf16[112,512]{1,0:T(8,128)(2,1)S(1)}, bf16[112,512]{1,0:T(8,128)(2,1)S(1)}, u32[]{:S(2)}, u32[]{:S(2)}) collective-permute-start(bf16[112,512]{1,0:T(8,128)(2,1)S(1)} %get-tuple-element.249), channel_id=1, source_target_pairs={{0,4},{1,5},{2,6},{3,7},{4,0},{5,1},{6,2},{7,3},{8,12},{9,13},{10,... | collective-permute-start | bytes 344072 | tf_op jit(solution)/shard_map/ppermute | solution.py:775
  136.7 5.5 %input_gradients.3 = (f32[768,512]{1,0:T(8,128)S(1)}, bf16[768,512]{1,0:T(8,128)(2,1)S(1)}) custom-call(f32[2,1536]{1,0:T(2,128)S(1)} %copy-done.19, bf16[1536,512]{1,0:T(8,128)(2,1)} %get-tuple-element.151.gk_hbm, bf16[1536,512]{1,0:T(8,128)(2,1)} %get-tuple-element.152.gv_hbm, bf16[8,64,384]{2,1,0:T(8,128)(2,1)} %get-tuple-element.153.gq_hbm, ...), custom_call_target="tpu_custom_call" | custom-call | flops 4831838208 | bytes 8388608 | tf_op jit(solution)/shard_map/input_gradients/pallas_call | solution.py:745
  142.3 3.5 %collective-permute-done.28 = bf16[112,512]{1,0:T(8,128)(2,1)S(1)} collective-permute-done((bf16[112,512]{1,0:T(8,128)(2,1)S(1)}, bf16[112,512]{1,0:T(8,128)(2,1)S(1)}, u32[]{:S(2)}, u32[]{:S(2)}) %collective-permute-start.28) | collective-permute-done | bytes 114720 | tf_op jit(solution)/shard_map/ppermute | solution.py:775
  145.9 2.4 %collective-permute-start.30 = (bf16[2,48,512]{2,1,0:T(8,128)(2,1)S(1)}, bf16[2,48,512]{2,1,0:T(8,128)(2,1)S(1)}, u32[]{:S(2)}, u32[]{:S(2)}) collective-permute-start(bf16[2,48,512]{2,1,0:T(8,128)(2,1)S(1)} %fusion.2), channel_id=1, source_target_pairs={{0,2},{1,3},{2,0},{3,1},{4,6},{5,7},{6,4},{7,5},{8,10},{9,11},{10,... | collective-permute-start | bytes 294920 | tf_op jit(solution)/shard_map/ppermute | solution.py:775
  153.9 2.7 %collective-permute-start.31 = (bf16[2,48,512]{2,1,0:T(8,128)(2,1)S(1)}, bf16[2,48,512]{2,1,0:T(8,128)(2,1)S(1)}, u32[]{:S(2)}, u32[]{:S(2)}) collective-permute-start(bf16[2,48,512]{2,1,0:T(8,128)(2,1)S(1)} %fusion.2), channel_id=1, source_target_pairs={{0,4},{1,5},{2,6},{3,7},{4,0},{5,1},{6,2},{7,3},{8,12},{9,13},{10,... | collective-permute-start | bytes 294920 | tf_op jit(solution)/shard_map/ppermute | solution.py:775
  156.7 5.8 %collective-permute-done.31 = bf16[2,48,512]{2,1,0:T(8,128)(2,1)S(1)} collective-permute-done((bf16[2,48,512]{2,1,0:T(8,128)(2,1)S(1)}, bf16[2,48,512]{2,1,0:T(8,128)(2,1)S(1)}, u32[]{:S(2)}, u32[]{:S(2)}) %collective-permute-start.31) | collective-permute-done | bytes 98336 | tf_op jit(solution)/shard_map/ppermute | solution.py:775
  162.4 2.4 %collective-permute-start.32 = (bf16[2,48,512]{2,1,0:T(8,128)(2,1)S(1)}, bf16[2,48,512]{2,1,0:T(8,128)(2,1)S(1)}, u32[]{:S(2)}, u32[]{:S(2)}) collective-permute-start(bf16[2,48,512]{2,1,0:T(8,128)(2,1)S(1)} %fusion.2), channel_id=1, source_target_pairs={{0,6},{1,7},{2,4},{3,5},{4,2},{5,3},{6,0},{7,1},{8,14},{9,15},{10,... | collective-permute-start | bytes 294920 | tf_op jit(solution)/shard_map/ppermute | solution.py:775
  164.9 4.0 %collective-permute-done.32 = bf16[2,48,512]{2,1,0:T(8,128)(2,1)S(1)} collective-permute-done((bf16[2,48,512]{2,1,0:T(8,128)(2,1)S(1)}, bf16[2,48,512]{2,1,0:T(8,128)(2,1)S(1)}, u32[]{:S(2)}, u32[]{:S(2)}) %collective-permute-start.32) | collective-permute-done | bytes 98336 | tf_op jit(solution)/shard_map/ppermute | solution.py:775
  169.1 3.4 %collective-permute-start.39 = (bf16[2,192,512]{2,1,0:T(8,128)(2,1)S(1)}, bf16[2,192,512]{2,1,0:T(8,128)(2,1)S(1)}, u32[]{:S(2)}, u32[]{:S(2)}) collective-permute-start(bf16[2,192,512]{2,1,0:T(8,128)(2,1)S(1)} %pad_maximum_fusion.11), channel_id=1, source_target_pairs={{0,24},{8,16},{16,8},{24,0},{1,25},{9,17},{17,9},{25,1},{2,26},{10... | collective-permute-start | bytes 1179656 | tf_op jit(solution)/shard_map/ppermute | solution.py:775
  176.9 5.6 %collective-permute-done.39 = bf16[2,192,512]{2,1,0:T(8,128)(2,1)S(1)} collective-permute-done((bf16[2,192,512]{2,1,0:T(8,128)(2,1)S(1)}, bf16[2,192,512]{2,1,0:T(8,128)(2,1)S(1)}, u32[]{:S(2)}, u32[]{:S(2)}) %collective-permute-start.39) | collective-permute-done | bytes 393248 | tf_op jit(solution)/shard_map/ppermute | solution.py:775
  182.6 7.4 %collective-permute-done.40 = bf16[2,192,512]{2,1,0:T(8,128)(2,1)S(1)} collective-permute-done((bf16[2,192,512]{2,1,0:T(8,128)(2,1)S(1)}, bf16[2,192,512]{2,1,0:T(8,128)(2,1)S(1)}, u32[]{:S(2)}, u32[]{:S(2)}) %collective-permute-start.40) | collective-permute-done | bytes 393248 | tf_op jit(solution)/shard_map/ppermute | solution.py:775
  191.4 2.8 %collective-permute-done.42.far_ref = bf16[2,768,512]{2,1,0:T(8,128)(2,1)S(1)} collective-permute-done((bf16[2,768,512]{2,1,0:T(8,128)(2,1)S(1)}, bf16[2,768,512]{2,1,0:T(8,128)(2,1)S(1)}, u32[]{:S(2)}, u32[]{:S(2)}) %collective-permute-start.42) | collective-permute-done | bytes 1572896 | tf_op jit(solution)/shard_map/ppermute | solution.py:775
  194.2 3.5 %finish.1 = (f32[512,512]{1,0:T(8,128)}, f32[512,512]{1,0:T(8,128)}, f32[512,512]{1,0:T(8,128)}, f32[512,512]{1,0:T(8,128)}, f32[512,512]{1,0:T(8,128)}, /*index=5*/f32[512,512]{1,0:T(8,128)}) custom-call(s32[3]{0:T(128)S(1)} %copy-done.21, bf16[2,768,512]{2,1,0:T(8,128)(2,1)S(1)} %pad_maximum_fusion.1.near_ref, ...), custom_call_target="tpu_custom_call" | custom-call | tf_op jit(solution)/shard_map/finish/pallas_call | solution.py:875
  (244 shorter events, 39.2 us)
Async XLA Ops:
  0.8 11.9 %collective-permute-start = (s32[3,1536]{1,0:T(4,128)}, s32[3,1536]{1,0:T(4,128)S(1)}, u32[]{:S(2)}, u32[]{:S(2)}) collective-permute-start(s32[3,1536]{1,0:T(4,128)} %near_ref.1), channel_id=1, source_target_pairs={{0,1},{1,0},{2,3},{3,2},{4,5},{5,4},{6,7},{7,6},{8,9},{9,8},{10,11... | collective-permute-start | bytes 55304 | tf_op jit(solution)/shard_map/ppermute | solution.py:775
  3.5 12.3 %collective-permute-start.1 = (bf16[192,512]{1,0:T(8,128)(2,1)}, bf16[192,512]{1,0:T(8,128)(2,1)S(1)}, u32[]{:S(2)}, u32[]{:S(2)}) collective-permute-start(bf16[192,512]{1,0:T(8,128)(2,1)} %get-tuple-element.188), channel_id=1, source_target_pairs={{0,0},{1,16},{2,2},{3,18},{4,4},{5,20},{6,6},{7,22},{8,8},{9,24},{... | collective-permute-start | bytes 589832 | tf_op jit(solution)/shard_map/ppermute | solution.py:949
  5.1 10.7 %collective-permute-start.2 = (bf16[192,512]{1,0:T(8,128)(2,1)}, bf16[192,512]{1,0:T(8,128)(2,1)}, u32[]{:S(2)}, u32[]{:S(2)}) collective-permute-start(bf16[192,512]{1,0:T(8,128)(2,1)} %get-tuple-element.187), channel_id=1, source_target_pairs={{0,1},{1,17},{2,3},{3,19},{4,5},{5,21},{6,7},{7,23},{8,9},{9,25},{... | collective-permute-start | bytes 589832 | tf_op jit(solution)/shard_map/ppermute | solution.py:949
  9.8 9.8 %collective-permute-start.4 = (bf16[192,512]{1,0:T(8,128)(2,1)}, bf16[192,512]{1,0:T(8,128)(2,1)}, u32[]{:S(2)}, u32[]{:S(2)}) collective-permute-start(bf16[192,512]{1,0:T(8,128)(2,1)} %get-tuple-element.186), channel_id=1, source_target_pairs={{0,9},{1,25},{2,11},{3,27},{4,13},{5,29},{6,15},{7,31},{8,1},{9,17... | collective-permute-start | bytes 589832 | tf_op jit(solution)/shard_map/ppermute | solution.py:949
  20.9 18.4 %collective-permute-start.6 = (bf16[192,512]{1,0:T(8,128)(2,1)S(1)}, bf16[192,512]{1,0:T(8,128)(2,1)S(1)}, u32[]{:S(2)}, u32[]{:S(2)}) collective-permute-start(bf16[192,512]{1,0:T(8,128)(2,1)S(1)} %get-tuple-element.102), channel_id=1, source_target_pairs={{0,0},{1,16},{2,2},{3,18},{4,4},{5,20},{6,6},{7,22},{8,8},{9,24},{... | collective-permute-start | bytes 589832 | tf_op jit(solution)/shard_map/ppermute | solution.py:955
  21.6 17.7 %collective-permute-start.7 = (bf16[192,512]{1,0:T(8,128)(2,1)S(1)}, bf16[192,512]{1,0:T(8,128)(2,1)S(1)}, u32[]{:S(2)}, u32[]{:S(2)}) collective-permute-start(bf16[192,512]{1,0:T(8,128)(2,1)S(1)} %get-tuple-element.103), channel_id=1, source_target_pairs={{0,1},{1,17},{2,3},{3,19},{4,5},{5,21},{6,7},{7,23},{8,9},{9,25},{... | collective-permute-start | bytes 589832 | tf_op jit(solution)/shard_map/ppermute | solution.py:955
  23.3 15.9 %collective-permute-start.8 = (bf16[192,512]{1,0:T(8,128)(2,1)S(1)}, bf16[192,512]{1,0:T(8,128)(2,1)S(1)}, u32[]{:S(2)}, u32[]{:S(2)}) collective-permute-start(bf16[192,512]{1,0:T(8,128)(2,1)S(1)} %get-tuple-element.104), channel_id=1, source_target_pairs={{0,8},{1,24},{2,10},{3,26},{4,12},{5,28},{6,14},{7,30},{8,0},{9,16... | collective-permute-start | bytes 589832 | tf_op jit(solution)/shard_map/ppermute | solution.py:955
  25.2 14.1 %collective-permute-start.9 = (bf16[192,512]{1,0:T(8,128)(2,1)S(1)}, bf16[192,512]{1,0:T(8,128)(2,1)S(1)}, u32[]{:S(2)}, u32[]{:S(2)}) collective-permute-start(bf16[192,512]{1,0:T(8,128)(2,1)S(1)} %get-tuple-element.105), channel_id=1, source_target_pairs={{0,9},{1,25},{2,11},{3,27},{4,13},{5,29},{6,15},{7,31},{8,1},{9,17... | collective-permute-start | bytes 589832 | tf_op jit(solution)/shard_map/ppermute | solution.py:955
  40.4 15.8 %collective-permute-start.11 = (bf16[2,192,512]{2,1,0:T(8,128)(2,1)S(1)}, bf16[2,192,512]{2,1,0:T(8,128)(2,1)S(1)}, u32[]{:S(2)}, u32[]{:S(2)}) collective-permute-start(bf16[2,192,512]{2,1,0:T(8,128)(2,1)S(1)} %copy-done.28), channel_id=1, source_target_pairs={{0,0},{1,16},{2,2},{3,18},{4,4},{5,20},{6,6},{7,22},{8,8},{9,24},{... | collective-permute-start | bytes 1179656 | tf_op jit(solution)/shard_map/ppermute | solution.py:957
  41.1 17.4 %collective-permute-start.12 = (bf16[2,192,512]{2,1,0:T(8,128)(2,1)S(1)}, bf16[2,192,512]{2,1,0:T(8,128)(2,1)S(1)}, u32[]{:S(2)}, u32[]{:S(2)}) collective-permute-start(bf16[2,192,512]{2,1,0:T(8,128)(2,1)S(1)} %copy-done.26), channel_id=1, source_target_pairs={{0,1},{1,17},{2,3},{3,19},{4,5},{5,21},{6,7},{7,23},{8,9},{9,25},{... | collective-permute-start | bytes 1179656 | tf_op jit(solution)/shard_map/ppermute | solution.py:957
  43.0 13.1 %collective-permute-start.13 = (bf16[1,192,512]{2,1,0:T(8,128)(2,1)}, bf16[1,192,512]{2,1,0:T(8,128)(2,1)S(1)}, u32[]{:S(2)}, u32[]{:S(2)}) collective-permute-start(bf16[1,192,512]{2,1,0:T(8,128)(2,1)} %copy-done.31), channel_id=1, source_target_pairs={{0,8},{1,24},{2,10},{3,26},{4,12},{5,28},{6,14},{7,30},{8,0},{9,16... | collective-permute-start | bytes 589832 | tf_op jit(solution)/shard_map/ppermute | solution.py:957
  44.8 11.4 %collective-permute-start.14 = (bf16[1,192,512]{2,1,0:T(8,128)(2,1)S(1)}, bf16[1,192,512]{2,1,0:T(8,128)(2,1)S(1)}, u32[]{:S(2)}, u32[]{:S(2)}) collective-permute-start(bf16[1,192,512]{2,1,0:T(8,128)(2,1)S(1)} %copy-done.30), channel_id=1, source_target_pairs={{0,9},{1,25},{2,11},{3,27},{4,13},{5,29},{6,15},{7,31},{8,1},{9,17... | collective-permute-start | bytes 589832 | tf_op jit(solution)/shard_map/ppermute | solution.py:957
  72.4 23.5 %collective-permute-start.19 = (bf16[784,512]{1,0:T(8,128)(2,1)S(1)}, bf16[784,512]{1,0:T(8,128)(2,1)S(1)}, u32[]{:S(2)}, u32[]{:S(2)}) collective-permute-start(bf16[784,512]{1,0:T(8,128)(2,1)S(1)} %get-tuple-element.134), channel_id=1, source_target_pairs={{0,1},{1,0},{2,3},{3,2},{4,5},{5,4},{6,7},{7,6},{8,9},{9,8},{10,11... | collective-permute-start | bytes 2408456 | tf_op jit(solution)/shard_map/ppermute | solution.py:775
  72.6 22.8 %collective-permute-start.15 = (bf16[1,192,512]{2,1,0:T(8,128)(2,1)S(1)}, bf16[1,192,512]{2,1,0:T(8,128)(2,1)S(1)}, u32[]{:S(2)}, u32[]{:S(2)}) collective-permute-start(bf16[1,192,512]{2,1,0:T(8,128)(2,1)S(1)} %get-tuple-element.220), channel_id=1, source_target_pairs={{9,0},{25,1},{11,2},{27,3},{13,4},{29,5},{15,6},{31,7},{1,8},{17,9... | collective-permute-start | bytes 589832 | tf_op jit(solution)/shard_map/ppermute | solution.py:991
  73.6 21.8 %collective-permute-start.16 = (bf16[1,192,512]{2,1,0:T(8,128)(2,1)S(1)}, bf16[1,192,512]{2,1,0:T(8,128)(2,1)S(1)}, u32[]{:S(2)}, u32[]{:S(2)}) collective-permute-start(bf16[1,192,512]{2,1,0:T(8,128)(2,1)S(1)} %get-tuple-element.223), channel_id=1, source_target_pairs={{8,0},{24,1},{10,2},{26,3},{12,4},{28,5},{14,6},{30,7},{0,8},{16,9... | collective-permute-start | bytes 589832 | tf_op jit(solution)/shard_map/ppermute | solution.py:991
  74.5 20.9 %collective-permute-start.17 = (bf16[2,192,512]{2,1,0:T(8,128)(2,1)S(1)}, bf16[2,192,512]{2,1,0:T(8,128)(2,1)S(1)}, u32[]{:S(2)}, u32[]{:S(2)}) collective-permute-start(bf16[2,192,512]{2,1,0:T(8,128)(2,1)S(1)} %pad_maximum_fusion.4), channel_id=1, source_target_pairs={{1,0},{17,1},{3,2},{19,3},{5,4},{21,5},{7,6},{23,7},{9,8},{25,9},{... | collective-permute-start | bytes 1179656 | tf_op jit(solution)/shard_map/ppermute | solution.py:991
  76.1 19.3 %collective-permute-start.18 = (bf16[2,192,512]{2,1,0:T(8,128)(2,1)S(1)}, bf16[2,192,512]{2,1,0:T(8,128)(2,1)S(1)}, u32[]{:S(2)}, u32[]{:S(2)}) collective-permute-start(bf16[2,192,512]{2,1,0:T(8,128)(2,1)S(1)} %pad_maximum_fusion.5), channel_id=1, source_target_pairs={{0,0},{16,1},{2,2},{18,3},{4,4},{20,5},{6,6},{22,7},{8,8},{24,9},{... | collective-permute-start | bytes 1179656 | tf_op jit(solution)/shard_map/ppermute | solution.py:991
  96.4 17.2 %collective-permute-start.20 = (bf16[208,512]{1,0:T(8,128)(2,1)S(1)}, bf16[208,512]{1,0:T(8,128)(2,1)S(1)}, u32[]{:S(2)}, u32[]{:S(2)}) collective-permute-start(bf16[208,512]{1,0:T(8,128)(2,1)S(1)} %get-tuple-element.254), channel_id=1, source_target_pairs={{0,8},{8,0},{16,24},{24,16},{1,9},{9,1},{17,25},{25,17},{2,10},{10... | collective-permute-start | bytes 638984 | tf_op jit(solution)/shard_map/ppermute | solution.py:775
  98.1 15.6 %collective-permute-start.21 = (bf16[208,512]{1,0:T(8,128)(2,1)S(1)}, bf16[208,512]{1,0:T(8,128)(2,1)S(1)}, u32[]{:S(2)}, u32[]{:S(2)}) collective-permute-start(bf16[208,512]{1,0:T(8,128)(2,1)S(1)} %get-tuple-element.256), channel_id=1, source_target_pairs={{0,16},{8,24},{16,0},{24,8},{1,17},{9,25},{17,1},{25,9},{2,18},{10... | collective-permute-start | bytes 638984 | tf_op jit(solution)/shard_map/ppermute | solution.py:775
  99.5 14.1 %collective-permute-start.22 = (bf16[208,512]{1,0:T(8,128)(2,1)S(1)}, bf16[208,512]{1,0:T(8,128)(2,1)S(1)}, u32[]{:S(2)}, u32[]{:S(2)}) collective-permute-start(bf16[208,512]{1,0:T(8,128)(2,1)S(1)} %get-tuple-element.255), channel_id=1, source_target_pairs={{0,24},{8,16},{16,8},{24,0},{1,25},{9,17},{17,9},{25,1},{2,26},{10... | collective-permute-start | bytes 638984 | tf_op jit(solution)/shard_map/ppermute | solution.py:775
  120.1 11.8 %collective-permute-start.25 = (bf16[208,512]{1,0:T(8,128)(2,1)S(1)}, bf16[208,512]{1,0:T(8,128)(2,1)S(1)}, u32[]{:S(2)}, u32[]{:S(2)}) collective-permute-start(bf16[208,512]{1,0:T(8,128)(2,1)S(1)} %get-tuple-element.253), channel_id=1, source_target_pairs={{0,16},{8,24},{16,0},{24,8},{1,17},{9,25},{17,1},{25,9},{2,18},{10... | collective-permute-start | bytes 638984 | tf_op jit(solution)/shard_map/ppermute | solution.py:775
  121.2 10.7 %collective-permute-start.26 = (bf16[208,512]{1,0:T(8,128)(2,1)S(1)}, bf16[208,512]{1,0:T(8,128)(2,1)S(1)}, u32[]{:S(2)}, u32[]{:S(2)}) collective-permute-start(bf16[208,512]{1,0:T(8,128)(2,1)S(1)} %get-tuple-element.252), channel_id=1, source_target_pairs={{0,24},{8,16},{16,8},{24,0},{1,25},{9,17},{17,9},{25,1},{2,26},{10... | collective-permute-start | bytes 638984 | tf_op jit(solution)/shard_map/ppermute | solution.py:775
  132.1 16.2 %collective-permute-start.33 = (bf16[768,512]{1,0:T(8,128)(2,1)S(1)}, bf16[768,512]{1,0:T(8,128)(2,1)S(1)}, u32[]{:S(2)}, u32[]{:S(2)}) collective-permute-start(bf16[768,512]{1,0:T(8,128)(2,1)S(1)} %get-tuple-element.163), channel_id=1, source_target_pairs={{0,1},{1,0},{2,3},{3,2},{4,5},{5,4},{6,7},{7,6},{8,9},{9,8},{10,11... | collective-permute-start | bytes 2359304 | tf_op jit(solution)/shard_map/ppermute | solution.py:775
  132.3 10.0 %collective-permute-start.27 = (bf16[112,512]{1,0:T(8,128)(2,1)S(1)}, bf16[112,512]{1,0:T(8,128)(2,1)S(1)}, u32[]{:S(2)}, u32[]{:S(2)}) collective-permute-start(bf16[112,512]{1,0:T(8,128)(2,1)S(1)} %get-tuple-element.250), channel_id=1, source_target_pairs={{0,2},{1,3},{2,0},{3,1},{4,6},{5,7},{6,4},{7,5},{8,10},{9,11},{10,... | collective-permute-start | bytes 344072 | tf_op jit(solution)/shard_map/ppermute | solution.py:775
  133.9 11.8 %collective-permute-start.28 = (bf16[112,512]{1,0:T(8,128)(2,1)S(1)}, bf16[112,512]{1,0:T(8,128)(2,1)S(1)}, u32[]{:S(2)}, u32[]{:S(2)}) collective-permute-start(bf16[112,512]{1,0:T(8,128)(2,1)S(1)} %get-tuple-element.249), channel_id=1, source_target_pairs={{0,4},{1,5},{2,6},{3,7},{4,0},{5,1},{6,2},{7,3},{8,12},{9,13},{10,... | collective-permute-start | bytes 344072 | tf_op jit(solution)/shard_map/ppermute | solution.py:775
  149.1 19.8 %collective-permute-start.38 = (bf16[2,192,512]{2,1,0:T(8,128)(2,1)S(1)}, bf16[2,192,512]{2,1,0:T(8,128)(2,1)S(1)}, u32[]{:S(2)}, u32[]{:S(2)}) collective-permute-start(bf16[2,192,512]{2,1,0:T(8,128)(2,1)S(1)} %pad_maximum_fusion.10), channel_id=1, source_target_pairs={{9,0},{25,1},{11,2},{27,3},{13,4},{29,5},{15,6},{31,7},{1,8},{17,9... | collective-permute-start | bytes 1179656 | tf_op jit(solution)/shard_map/ppermute | solution.py:1025
  150.3 18.7 %collective-permute-start.37 = (bf16[2,192,512]{2,1,0:T(8,128)(2,1)S(1)}, bf16[2,192,512]{2,1,0:T(8,128)(2,1)S(1)}, u32[]{:S(2)}, u32[]{:S(2)}) collective-permute-start(bf16[2,192,512]{2,1,0:T(8,128)(2,1)S(1)} %pad_maximum_fusion.9), channel_id=1, source_target_pairs={{8,0},{24,1},{10,2},{26,3},{12,4},{28,5},{14,6},{30,7},{0,8},{16,9... | collective-permute-start | bytes 1179656 | tf_op jit(solution)/shard_map/ppermute | solution.py:1025
  151.6 17.4 %collective-permute-start.36 = (bf16[2,192,512]{2,1,0:T(8,128)(2,1)S(1)}, bf16[2,192,512]{2,1,0:T(8,128)(2,1)S(1)}, u32[]{:S(2)}, u32[]{:S(2)}) collective-permute-start(bf16[2,192,512]{2,1,0:T(8,128)(2,1)S(1)} %pad_maximum_fusion.8), channel_id=1, source_target_pairs={{1,0},{17,1},{3,2},{19,3},{5,4},{21,5},{7,6},{23,7},{9,8},{25,9},{... | collective-permute-start | bytes 1179656 | tf_op jit(solution)/shard_map/ppermute | solution.py:1025
  152.5 16.5 %collective-permute-start.35 = (bf16[2,192,512]{2,1,0:T(8,128)(2,1)S(1)}, bf16[2,192,512]{2,1,0:T(8,128)(2,1)}, u32[]{:S(2)}, u32[]{:S(2)}) collective-permute-start(bf16[2,192,512]{2,1,0:T(8,128)(2,1)S(1)} %pad_maximum_fusion.7), channel_id=1, source_target_pairs={{0,0},{16,1},{2,2},{18,3},{4,4},{20,5},{6,6},{22,7},{8,8},{24,9},{... | collective-permute-start | bytes 1179656 | tf_op jit(solution)/shard_map/ppermute | solution.py:1025
  169.1 13.5 %collective-permute-start.39 = (bf16[2,192,512]{2,1,0:T(8,128)(2,1)S(1)}, bf16[2,192,512]{2,1,0:T(8,128)(2,1)S(1)}, u32[]{:S(2)}, u32[]{:S(2)}) collective-permute-start(bf16[2,192,512]{2,1,0:T(8,128)(2,1)S(1)} %pad_maximum_fusion.11), channel_id=1, source_target_pairs={{0,24},{8,16},{16,8},{24,0},{1,25},{9,17},{17,9},{25,1},{2,26},{10... | collective-permute-start | bytes 1179656 | tf_op jit(solution)/shard_map/ppermute | solution.py:775
  172.5 17.4 %collective-permute-start.40 = (bf16[2,192,512]{2,1,0:T(8,128)(2,1)S(1)}, bf16[2,192,512]{2,1,0:T(8,128)(2,1)S(1)}, u32[]{:S(2)}, u32[]{:S(2)}) collective-permute-start(bf16[2,192,512]{2,1,0:T(8,128)(2,1)S(1)} %pad_maximum_fusion.11), channel_id=1, source_target_pairs={{0,16},{8,24},{16,0},{24,8},{1,17},{9,25},{17,1},{25,9},{2,18},{10... | collective-permute-start | bytes 1179656 | tf_op jit(solution)/shard_map/ppermute | solution.py:775
  172.5 17.4 %collective-permute-start.41 = (bf16[2,192,512]{2,1,0:T(8,128)(2,1)S(1)}, bf16[2,192,512]{2,1,0:T(8,128)(2,1)S(1)}, u32[]{:S(2)}, u32[]{:S(2)}) collective-permute-start(bf16[2,192,512]{2,1,0:T(8,128)(2,1)S(1)} %pad_maximum_fusion.11), channel_id=1, source_target_pairs={{0,8},{8,0},{16,24},{24,16},{1,9},{9,1},{17,25},{25,17},{2,10},{10... | collective-permute-start | bytes 1179656 | tf_op jit(solution)/shard_map/ppermute | solution.py:775
  (67 other events, 541.9 us)
where the time goes:
time: 202 us; the launch traced here: 198 us
  Pallas kernels  86.5 us (43%)
  starting transfers between devices  51.1 us (25%)
  waiting for transfers between devices  41.5 us (21%)
  local copies, waits for them, and re-layouts  8.69 us (4%)
  other arithmetic  7.75 us (4%)
  between operations  2.58 us (1%)
    ppermute x23, waiting for transfers between devices, exchange(): return lax.ppermute(piece, axis, [(i, i ^ partner) for i in range(count)])  35.3 us
    pallas_call x2, Pallas kernels, attention_backward(): pl.pallas_call(functools.partial(backward_kernel, sizes_of(length), bool(...  32.1 us
    ppermute x23, starting transfers between devices, exchange(): return lax.ppermute(piece, axis, [(i, i ^ partner) for i in range(count)])  25.4 us
    pallas_call x2, Pallas kernels, attention_forward(): pl.pallas_call(functools.partial(forward_kernel, sizes_of(length), cell),...  23.4 us
    pallas_call x1, Pallas kernels, middle(): pl.pallas_call(middle_kernel, grid=(steps + 1,), out_shape=(*out_shape, j...  13.8 us
    pallas_call x2, Pallas kernels, input_gradients(): pl.pallas_call(functools.partial(inputs_kernel, sizes_of(length), cell, l...  11.6 us
    ppermute x8, starting transfers between devices, body(): lax.ppermute(sent, axes, route(*ij))  10.5 us
    ppermute x4, starting transfers between devices, body(): lax.ppermute(cell_of(near_rows(tokens, j), i)[0], axes, route(i, j))  6.25 us
  transfers between devices with their start and end apart: 43, of which 12 were waited for; matrix products, arithmetic and copies ran while one was open for 5% of the time, Pallas kernels for 34%

commit v1 on v0

--- a/solution.py
+++ b/solution.py
@@ -22,7 +22,6 @@
 FORWARD_BYTES = 20 * 1024 * 1024
 MIDDLE_BYTES = 20 * 1024 * 1024
 BACKWARD_BYTES = 40 * 1024 * 1024
-UNROLL = 8
 
 
 def dot(a, b, dims=NN):
@@ -52,15 +51,16 @@
         padded[h] = jnp.concatenate([part, blank] if h % 2 == 0 else [blank, part], 0)
 
 
+def pair_of(head, wide):
+    start = head // 2 * wide
+    return pl.ds(start if isinstance(head, int) else pl.multiple_of(start, wide), wide)
+
+
 def over_heads(run, heads, rows, common):
     if common:
 
-        def step(i, carry):
-            for t in range(UNROLL):
-                run(UNROLL * i + t, 0, rows)
-            return carry
-
-        lax.fori_loop(0, heads // UNROLL, step, 0)
+        for h in range(heads):
+            run(h, 0, rows)
     else:
         wide = 128
         chunks = rows // wide
@@ -230,7 +230,7 @@
         )
 
         def head(h, at, wide):
-            pair = pl.ds(pl.multiple_of(h // 2 * 2 * size, 2 * size), 2 * size)
+            pair = pair_of(h, 2 * size)
             raw = dot(keys_ref[0:n, pair], q_s[h, :, pl.ds(at, wide)])
             seen = lax.broadcasted_iota(jnp.int32, raw.shape, 0) < count
             scores = jnp.where(seen, raw * scale, NONE)
@@ -539,7 +539,7 @@
 
         def head(h, at, wide):
             here = pl.ds(at, wide)
-            pair = pl.ds(pl.multiple_of(h // 2 * 2 * size, 2 * size), 2 * size)
+            pair = pair_of(h, 2 * size)
             k_pair = keys_ref[0:n, pair]
             v_pair = v_s[0:n, pair]
             q_full = q_s[h, :, here]

time: 202 us -> 202 us (level)
  no operation moved by 1% of the time
where the time goes in v1:
time: 202 us; the launch traced here: 198 us
  Pallas kernels  86.5 us (43%)
  starting transfers between devices  51.1 us (25%)
  waiting for transfers between devices  41.5 us (21%)
  local copies, waits for them, and re-layouts  8.69 us (4%)
  other arithmetic  7.75 us (4%)
  between operations  2.58 us (1%)
    ppermute x23, waiting for transfers between devices, exchange(): return lax.ppermute(piece, axis, [(i, i ^ partner) for i in range(count)])  35.3 us
    pallas_call x2, Pallas kernels, attention_backward(): pl.pallas_call(functools.partial(backward_kernel, sizes_of(length), bool(...  32.1 us
    ppermute x23, starting transfers between devices, exchange(): return lax.ppermute(piece, axis, [(i, i ^ partner) for i in range(count)])  25.4 us
    pallas_call x2, Pallas kernels, attention_forward(): pl.pallas_call(functools.partial(forward_kernel, sizes_of(length), cell),...  23.4 us
    pallas_call x1, Pallas kernels, middle(): pl.pallas_call(middle_kernel, grid=(steps + 1,), out_shape=(*out_shape, j...  13.8 us
    pallas_call x2, Pallas kernels, input_gradients(): pl.pallas_call(functools.partial(inputs_kernel, sizes_of(length), cell, l...  11.6 us
    ppermute x8, starting transfers between devices, body(): lax.ppermute(sent, axes, route(*ij))  10.5 us
    ppermute x4, starting transfers between devices, body(): lax.ppermute(cell_of(near_rows(tokens, j), i)[0], axes, route(i, j))  6.25 us
  transfers between devices with their start and end apart: 43, of which 12 were waited for; matrix products, arithmetic and copies ran while one was open for 5% of the time, Pallas kernels for 34%

profile of v1, /device:TPU:0, one launch (start us, length us, event | category | flops | bytes accessed | tf_op | source)
XLA Modules:
  0.0 198.2 jit_solution(6949949158843619057)
XLA Ops:
  1.3 2.2 %dynamic-slice_bitcast_fusion = (bf16[192,512]{1,0:T(8,128)(2,1)}, bf16[192,512]{1,0:T(8,128)(2,1)}, bf16[192,512]{1,0:T(8,128)(2,1)}, bf16[192,512]{1,0:T(8,128)(2,1)}) fusion(bf16[3,384,512]{2,1,0:T(8,128)(2,1)} %tokens_ref.1, s32[]{:T(128)S(6)} %select_n.349, s32[]{:T(128)S(6)} %select_n.347, s32[]{:T(128)S(6)} %select_n.343, s32[]{:T(128)S(6)} %select_n.345), kind=kLoop, calls=%fused_computation.58 | loop fusion | bytes 1572880 | tf_op jit(solution)/shard_map/squeeze | solution.py:949
  5.1 3.2 %collective-permute-start.2 = (bf16[192,512]{1,0:T(8,128)(2,1)}, bf16[192,512]{1,0:T(8,128)(2,1)}, u32[]{:S(2)}, u32[]{:S(2)}) collective-permute-start(bf16[192,512]{1,0:T(8,128)(2,1)} %get-tuple-element.187), channel_id=1, source_target_pairs={{0,1},{1,17},{2,3},{3,19},{4,5},{5,21},{6,7},{7,23},{8,9},{9,25},{... | collective-permute-start | bytes 589832 | tf_op jit(solution)/shard_map/ppermute | solution.py:949
  16.4 3.2 %collective-permute-done.4.refs_3_ = bf16[192,512]{1,0:T(8,128)(2,1)} collective-permute-done((bf16[192,512]{1,0:T(8,128)(2,1)}, bf16[192,512]{1,0:T(8,128)(2,1)}, u32[]{:S(2)}, u32[]{:S(2)}) %collective-permute-start.4) | collective-permute-done | bytes 196640 | tf_op jit(solution)/shard_map/ppermute | solution.py:949
  21.6 1.7 collective-permute-start.7
  23.3 1.9 collective-permute-start.8
  26.2 12.9 %attention_forward.2 = (bf16[8,64,768]{2,1,0:T(8,128)(2,1)S(1)}, f32[8,1,768]{2,1,0:T(1,128)S(1)}, f32[8,1,768]{2,1,0:T(1,128)S(1)}, bf16[8,64,768]{2,1,0:T(8,12...) custom-call(f32[2,1536]{1,0:T(2,128)S(1)} %get-tuple-element.100.ref, ...), custom_call_target="tpu_custom_call" | custom-call | flops 9663676416 | bytes 8388608 | tf_op jit(solution)/shard_map/attention_forward/pallas_call | solution.py:267
  41.1 2.0 %collective-permute-start.12 = (bf16[2,192,512]{2,1,0:T(8,128)(2,1)S(1)}, bf16[2,192,512]{2,1,0:T(8,128)(2,1)S(1)}, u32[]{:S(2)}, u32[]{:S(2)}) collective-permute-start(bf16[2,192,512]{2,1,0:T(8,128)(2,1)S(1)} %copy-done.26), channel_id=1, source_target_pairs={{0,1},{1,17},{2,3},{3,19},{4,5},{5,21},{6,7},{7,23},{8,9},{9,25},{... | collective-permute-start | bytes 1179656 | tf_op jit(solution)/shard_map/ppermute | solution.py:957
  43.0 1.7 collective-permute-start.13
  45.7 10.5 %attention_forward.3 = (bf16[8,64,384]{2,1,0:T(8,128)(2,1)S(1)}, f32[8,1,384]{2,1,0:T(1,128)S(1)}, f32[8,1,384]{2,1,0:T(1,128)S(1)}, bf16[8,64,384]{2,1,0:T(8,12...) custom-call(f32[2,1536]{1,0:T(2,128)S(1)} %copy-done.19, ...), custom_call_target="tpu_custom_call" | custom-call | flops 4831838208 | bytes 8388608 | tf_op jit(solution)/shard_map/attention_forward/pallas_call | solution.py:267
  56.2 2.2 %collective-permute-done.12.cot_1_ref = bf16[2,192,512]{2,1,0:T(8,128)(2,1)S(1)} collective-permute-done((bf16[2,192,512]{2,1,0:T(8,128)(2,1)S(1)}, bf16[2,192,512]{2,1,0:T(8,128)(2,1)S(1)}, u32[]{:S(2)}, u32[]{:S(2)}) %collective-permute-start.12) | collective-permute-done | bytes 393248 | tf_op jit(solution)/shard_map/ppermute | solution.py:957
  58.5 13.8 %middle.1 = (bf16[768,512]{1,0:T(8,128)(2,1)S(1)}, f32[768,512]{1,0:T(8,128)S(1)}, bf16[8,64,768]{2,1,0:T(8,128)(2,1)S(1)}, f32[8,1,768]{2,1,0:T(1,128)S(1)}, bf...) custom-call(s32[3]{0:T(128)S(1)} %copy-done.21, ...), custom_call_target="tpu_custom_call" | custom-call | flops 10871635968 | bytes 8388608 | tf_op jit(solution)/shard_map/middle/pallas_call | solution.py:442
  76.9 18.5 %attention_backward.2 = (bf16[1536,512]{1,0:T(8,128)(2,1)}, bf16[1536,512]{1,0:T(8,128)(2,1)}, bf16[8,64,768]{2,1,0:T(8,128)(2,1)}, bf16[8,64,768]{2,1,0:T(8,128...) custom-call(s32[3]{0:T(128)S(1)} %copy-done.21, f32[2,1536]{1,0:T(2,128)S(1)} %copy-done.19, ...), custom_call_target="tpu_custom_call" | custom-call | flops 18119393280 | bytes 16777216 | tf_op jit(solution)/shard_map/attention_backward/pallas_call | solution.py:645
  96.4 1.7 collective-permute-start.20
  100.0 13.6 %attention_backward.3 = (bf16[1536,512]{1,0:T(8,128)(2,1)}, bf16[1536,512]{1,0:T(8,128)(2,1)}, bf16[8,64,384]{2,1,0:T(8,128)(2,1)}, bf16[8,64,384]{2,1,0:T(8,128...) custom-call(s32[3]{0:T(128)S(1)} %copy-done.21, ...), custom_call_target="tpu_custom_call" | custom-call | flops 9059696640 | bytes 16777216 | tf_op jit(solution)/shard_map/attention_backward/pallas_call | solution.py:645
  114.5 2.3 %collective-permute-done.23 = bf16[784,512]{1,0:T(8,128)(2,1)} collective-permute-done((bf16[784,512]{1,0:T(8,128)(2,1)}, bf16[784,512]{1,0:T(8,128)(2,1)}, u32[]{:S(2)}, u32[]{:S(2)}) %collective-permute-start.23) | collective-permute-done | bytes 802848 | tf_op jit(solution)/shard_map/ppermute | solution.py:775
  118.4 1.8 collective-permute-start.24
  121.9 6.0 %input_gradients.2 = (f32[768,512]{1,0:T(8,128)S(1)}, bf16[768,512]{1,0:T(8,128)(2,1)S(1)}) custom-call(f32[2,1536]{1,0:T(2,128)S(1)} %copy-done.19, bf16[1536,512]{1,0:T(8,128)(2,1)} %get-tuple-element.140.gk_hbm, bf16[1536,512]{1,0:T(8,128)(2,1)} %get-tuple-element.141.gv_hbm, bf16[8,64,768]{2,1,0:T(8,128)(2,1)} %get-tuple-element.142.gq_hbm, ...), custom_call_target="tpu_custom_call" | custom-call | flops 4831838208 | bytes 8388608 | tf_op jit(solution)/shard_map/input_gradients/pallas_call | solution.py:745
  128.0 3.9 %collective-permute-done.25 = bf16[208,512]{1,0:T(8,128)(2,1)S(1)} collective-permute-done((bf16[208,512]{1,0:T(8,128)(2,1)S(1)}, bf16[208,512]{1,0:T(8,128)(2,1)S(1)}, u32[]{:S(2)}, u32[]{:S(2)}) %collective-permute-start.25) | collective-permute-done | bytes 213024 | tf_op jit(solution)/shard_map/ppermute | solution.py:775
  132.3 1.6 collective-permute-start.27
  133.9 2.6 %collective-permute-start.28 = (bf16[112,512]{1,0:T(8,128)(2,1)S(1)}, bf16[112,512]{1,0:T(8,128)(2,1)S(1)}, u32[]{:S(2)}, u32[]{:S(2)}) collective-permute-start(bf16[112,512]{1,0:T(8,128)(2,1)S(1)} %get-tuple-element.249), channel_id=1, source_target_pairs={{0,4},{1,5},{2,6},{3,7},{4,0},{5,1},{6,2},{7,3},{8,12},{9,13},{10,... | collective-permute-start | bytes 344072 | tf_op jit(solution)/shard_map/ppermute | solution.py:775
  136.7 5.5 %input_gradients.3 = (f32[768,512]{1,0:T(8,128)S(1)}, bf16[768,512]{1,0:T(8,128)(2,1)S(1)}) custom-call(f32[2,1536]{1,0:T(2,128)S(1)} %copy-done.19, bf16[1536,512]{1,0:T(8,128)(2,1)} %get-tuple-element.151.gk_hbm, bf16[1536,512]{1,0:T(8,128)(2,1)} %get-tuple-element.152.gv_hbm, bf16[8,64,384]{2,1,0:T(8,128)(2,1)} %get-tuple-element.153.gq_hbm, ...), custom_call_target="tpu_custom_call" | custom-call | flops 4831838208 | bytes 8388608 | tf_op jit(solution)/shard_map/input_gradients/pallas_call | solution.py:745
  142.3 3.5 %collective-permute-done.28 = bf16[112,512]{1,0:T(8,128)(2,1)S(1)} collective-permute-done((bf16[112,512]{1,0:T(8,128)(2,1)S(1)}, bf16[112,512]{1,0:T(8,128)(2,1)S(1)}, u32[]{:S(2)}, u32[]{:S(2)}) %collective-permute-start.28) | collective-permute-done | bytes 114720 | tf_op jit(solution)/shard_map/ppermute | solution.py:775
  145.9 2.4 %collective-permute-start.30 = (bf16[2,48,512]{2,1,0:T(8,128)(2,1)S(1)}, bf16[2,48,512]{2,1,0:T(8,128)(2,1)S(1)}, u32[]{:S(2)}, u32[]{:S(2)}) collective-permute-start(bf16[2,48,512]{2,1,0:T(8,128)(2,1)S(1)} %fusion.2), channel_id=1, source_target_pairs={{0,2},{1,3},{2,0},{3,1},{4,6},{5,7},{6,4},{7,5},{8,10},{9,11},{10,... | collective-permute-start | bytes 294920 | tf_op jit(solution)/shard_map/ppermute | solution.py:775
  153.9 2.7 %collective-permute-start.31 = (bf16[2,48,512]{2,1,0:T(8,128)(2,1)S(1)}, bf16[2,48,512]{2,1,0:T(8,128)(2,1)S(1)}, u32[]{:S(2)}, u32[]{:S(2)}) collective-permute-start(bf16[2,48,512]{2,1,0:T(8,128)(2,1)S(1)} %fusion.2), channel_id=1, source_target_pairs={{0,4},{1,5},{2,6},{3,7},{4,0},{5,1},{6,2},{7,3},{8,12},{9,13},{10,... | collective-permute-start | bytes 294920 | tf_op jit(solution)/shard_map/ppermute | solution.py:775
  156.7 5.8 %collective-permute-done.31 = bf16[2,48,512]{2,1,0:T(8,128)(2,1)S(1)} collective-permute-done((bf16[2,48,512]{2,1,0:T(8,128)(2,1)S(1)}, bf16[2,48,512]{2,1,0:T(8,128)(2,1)S(1)}, u32[]{:S(2)}, u32[]{:S(2)}) %collective-permute-start.31) | collective-permute-done | bytes 98336 | tf_op jit(solution)/shard_map/ppermute | solution.py:775
  162.4 2.4 %collective-permute-start.32 = (bf16[2,48,512]{2,1,0:T(8,128)(2,1)S(1)}, bf16[2,48,512]{2,1,0:T(8,128)(2,1)S(1)}, u32[]{:S(2)}, u32[]{:S(2)}) collective-permute-start(bf16[2,48,512]{2,1,0:T(8,128)(2,1)S(1)} %fusion.2), channel_id=1, source_target_pairs={{0,6},{1,7},{2,4},{3,5},{4,2},{5,3},{6,0},{7,1},{8,14},{9,15},{10,... | collective-permute-start | bytes 294920 | tf_op jit(solution)/shard_map/ppermute | solution.py:775
  164.9 4.0 %collective-permute-done.32 = bf16[2,48,512]{2,1,0:T(8,128)(2,1)S(1)} collective-permute-done((bf16[2,48,512]{2,1,0:T(8,128)(2,1)S(1)}, bf16[2,48,512]{2,1,0:T(8,128)(2,1)S(1)}, u32[]{:S(2)}, u32[]{:S(2)}) %collective-permute-start.32) | collective-permute-done | bytes 98336 | tf_op jit(solution)/shard_map/ppermute | solution.py:775
  169.1 3.4 %collective-permute-start.39 = (bf16[2,192,512]{2,1,0:T(8,128)(2,1)S(1)}, bf16[2,192,512]{2,1,0:T(8,128)(2,1)S(1)}, u32[]{:S(2)}, u32[]{:S(2)}) collective-permute-start(bf16[2,192,512]{2,1,0:T(8,128)(2,1)S(1)} %pad_maximum_fusion.11), channel_id=1, source_target_pairs={{0,24},{8,16},{16,8},{24,0},{1,25},{9,17},{17,9},{25,1},{2,26},{10... | collective-permute-start | bytes 1179656 | tf_op jit(solution)/shard_map/ppermute | solution.py:775
  176.9 5.6 %collective-permute-done.39 = bf16[2,192,512]{2,1,0:T(8,128)(2,1)S(1)} collective-permute-done((bf16[2,192,512]{2,1,0:T(8,128)(2,1)S(1)}, bf16[2,192,512]{2,1,0:T(8,128)(2,1)S(1)}, u32[]{:S(2)}, u32[]{:S(2)}) %collective-permute-start.39) | collective-permute-done | bytes 393248 | tf_op jit(solution)/shard_map/ppermute | solution.py:775
  182.6 7.4 %collective-permute-done.40 = bf16[2,192,512]{2,1,0:T(8,128)(2,1)S(1)} collective-permute-done((bf16[2,192,512]{2,1,0:T(8,128)(2,1)S(1)}, bf16[2,192,512]{2,1,0:T(8,128)(2,1)S(1)}, u32[]{:S(2)}, u32[]{:S(2)}) %collective-permute-start.40) | collective-permute-done | bytes 393248 | tf_op jit(solution)/shard_map/ppermute | solution.py:775
  191.4 2.8 %collective-permute-done.42.far_ref = bf16[2,768,512]{2,1,0:T(8,128)(2,1)S(1)} collective-permute-done((bf16[2,768,512]{2,1,0:T(8,128)(2,1)S(1)}, bf16[2,768,512]{2,1,0:T(8,128)(2,1)S(1)}, u32[]{:S(2)}, u32[]{:S(2)}) %collective-permute-start.42) | collective-permute-done | bytes 1572896 | tf_op jit(solution)/shard_map/ppermute | solution.py:775
  194.2 3.5 %finish.1 = (f32[512,512]{1,0:T(8,128)}, f32[512,512]{1,0:T(8,128)}, f32[512,512]{1,0:T(8,128)}, f32[512,512]{1,0:T(8,128)}, f32[512,512]{1,0:T(8,128)}, /*index=5*/f32[512,512]{1,0:T(8,128)}) custom-call(s32[3]{0:T(128)S(1)} %copy-done.21, bf16[2,768,512]{2,1,0:T(8,128)(2,1)S(1)} %pad_maximum_fusion.1.near_ref, ...), custom_call_target="tpu_custom_call" | custom-call | tf_op jit(solution)/shard_map/finish/pallas_call | solution.py:875
  (244 shorter events, 39.2 us)
Async XLA Ops:
  0.8 11.9 %collective-permute-start = (s32[3,1536]{1,0:T(4,128)}, s32[3,1536]{1,0:T(4,128)S(1)}, u32[]{:S(2)}, u32[]{:S(2)}) collective-permute-start(s32[3,1536]{1,0:T(4,128)} %near_ref.1), channel_id=1, source_target_pairs={{0,1},{1,0},{2,3},{3,2},{4,5},{5,4},{6,7},{7,6},{8,9},{9,8},{10,11... | collective-permute-start | bytes 55304 | tf_op jit(solution)/shard_map/ppermute | solution.py:775
  3.5 12.3 %collective-permute-start.1 = (bf16[192,512]{1,0:T(8,128)(2,1)}, bf16[192,512]{1,0:T(8,128)(2,1)S(1)}, u32[]{:S(2)}, u32[]{:S(2)}) collective-permute-start(bf16[192,512]{1,0:T(8,128)(2,1)} %get-tuple-element.188), channel_id=1, source_target_pairs={{0,0},{1,16},{2,2},{3,18},{4,4},{5,20},{6,6},{7,22},{8,8},{9,24},{... | collective-permute-start | bytes 589832 | tf_op jit(solution)/shard_map/ppermute | solution.py:949
  5.1 10.7 %collective-permute-start.2 = (bf16[192,512]{1,0:T(8,128)(2,1)}, bf16[192,512]{1,0:T(8,128)(2,1)}, u32[]{:S(2)}, u32[]{:S(2)}) collective-permute-start(bf16[192,512]{1,0:T(8,128)(2,1)} %get-tuple-element.187), channel_id=1, source_target_pairs={{0,1},{1,17},{2,3},{3,19},{4,5},{5,21},{6,7},{7,23},{8,9},{9,25},{... | collective-permute-start | bytes 589832 | tf_op jit(solution)/shard_map/ppermute | solution.py:949
  9.8 9.8 %collective-permute-start.4 = (bf16[192,512]{1,0:T(8,128)(2,1)}, bf16[192,512]{1,0:T(8,128)(2,1)}, u32[]{:S(2)}, u32[]{:S(2)}) collective-permute-start(bf16[192,512]{1,0:T(8,128)(2,1)} %get-tuple-element.186), channel_id=1, source_target_pairs={{0,9},{1,25},{2,11},{3,27},{4,13},{5,29},{6,15},{7,31},{8,1},{9,17... | collective-permute-start | bytes 589832 | tf_op jit(solution)/shard_map/ppermute | solution.py:949
  20.9 18.4 %collective-permute-start.6 = (bf16[192,512]{1,0:T(8,128)(2,1)S(1)}, bf16[192,512]{1,0:T(8,128)(2,1)S(1)}, u32[]{:S(2)}, u32[]{:S(2)}) collective-permute-start(bf16[192,512]{1,0:T(8,128)(2,1)S(1)} %get-tuple-element.102), channel_id=1, source_target_pairs={{0,0},{1,16},{2,2},{3,18},{4,4},{5,20},{6,6},{7,22},{8,8},{9,24},{... | collective-permute-start | bytes 589832 | tf_op jit(solution)/shard_map/ppermute | solution.py:955
  21.6 17.7 %collective-permute-start.7 = (bf16[192,512]{1,0:T(8,128)(2,1)S(1)}, bf16[192,512]{1,0:T(8,128)(2,1)S(1)}, u32[]{:S(2)}, u32[]{:S(2)}) collective-permute-start(bf16[192,512]{1,0:T(8,128)(2,1)S(1)} %get-tuple-element.103), channel_id=1, source_target_pairs={{0,1},{1,17},{2,3},{3,19},{4,5},{5,21},{6,7},{7,23},{8,9},{9,25},{... | collective-permute-start | bytes 589832 | tf_op jit(solution)/shard_map/ppermute | solution.py:955
  23.3 15.9 %collective-permute-start.8 = (bf16[192,512]{1,0:T(8,128)(2,1)S(1)}, bf16[192,512]{1,0:T(8,128)(2,1)S(1)}, u32[]{:S(2)}, u32[]{:S(2)}) collective-permute-start(bf16[192,512]{1,0:T(8,128)(2,1)S(1)} %get-tuple-element.104), channel_id=1, source_target_pairs={{0,8},{1,24},{2,10},{3,26},{4,12},{5,28},{6,14},{7,30},{8,0},{9,16... | collective-permute-start | bytes 589832 | tf_op jit(solution)/shard_map/ppermute | solution.py:955
  25.2 14.1 %collective-permute-start.9 = (bf16[192,512]{1,0:T(8,128)(2,1)S(1)}, bf16[192,512]{1,0:T(8,128)(2,1)S(1)}, u32[]{:S(2)}, u32[]{:S(2)}) collective-permute-start(bf16[192,512]{1,0:T(8,128)(2,1)S(1)} %get-tuple-element.105), channel_id=1, source_target_pairs={{0,9},{1,25},{2,11},{3,27},{4,13},{5,29},{6,15},{7,31},{8,1},{9,17... | collective-permute-start | bytes 589832 | tf_op jit(solution)/shard_map/ppermute | solution.py:955
  40.4 15.8 %collective-permute-start.11 = (bf16[2,192,512]{2,1,0:T(8,128)(2,1)S(1)}, bf16[2,192,512]{2,1,0:T(8,128)(2,1)S(1)}, u32[]{:S(2)}, u32[]{:S(2)}) collective-permute-start(bf16[2,192,512]{2,1,0:T(8,128)(2,1)S(1)} %copy-done.28), channel_id=1, source_target_pairs={{0,0},{1,16},{2,2},{3,18},{4,4},{5,20},{6,6},{7,22},{8,8},{9,24},{... | collective-permute-start | bytes 1179656 | tf_op jit(solution)/shard_map/ppermute | solution.py:957
  41.1 17.4 %collective-permute-start.12 = (bf16[2,192,512]{2,1,0:T(8,128)(2,1)S(1)}, bf16[2,192,512]{2,1,0:T(8,128)(2,1)S(1)}, u32[]{:S(2)}, u32[]{:S(2)}) collective-permute-start(bf16[2,192,512]{2,1,0:T(8,128)(2,1)S(1)} %copy-done.26), channel_id=1, source_target_pairs={{0,1},{1,17},{2,3},{3,19},{4,5},{5,21},{6,7},{7,23},{8,9},{9,25},{... | collective-permute-start | bytes 1179656 | tf_op jit(solution)/shard_map/ppermute | solution.py:957
  43.0 13.1 %collective-permute-start.13 = (bf16[1,192,512]{2,1,0:T(8,128)(2,1)}, bf16[1,192,512]{2,1,0:T(8,128)(2,1)S(1)}, u32[]{:S(2)}, u32[]{:S(2)}) collective-permute-start(bf16[1,192,512]{2,1,0:T(8,128)(2,1)} %copy-done.31), channel_id=1, source_target_pairs={{0,8},{1,24},{2,10},{3,26},{4,12},{5,28},{6,14},{7,30},{8,0},{9,16... | collective-permute-start | bytes 589832 | tf_op jit(solution)/shard_map/ppermute | solution.py:957
  44.8 11.4 %collective-permute-start.14 = (bf16[1,192,512]{2,1,0:T(8,128)(2,1)S(1)}, bf16[1,192,512]{2,1,0:T(8,128)(2,1)S(1)}, u32[]{:S(2)}, u32[]{:S(2)}) collective-permute-start(bf16[1,192,512]{2,1,0:T(8,128)(2,1)S(1)} %copy-done.30), channel_id=1, source_target_pairs={{0,9},{1,25},{2,11},{3,27},{4,13},{5,29},{6,15},{7,31},{8,1},{9,17... | collective-permute-start | bytes 589832 | tf_op jit(solution)/shard_map/ppermute | solution.py:957
  72.4 23.5 %collective-permute-start.19 = (bf16[784,512]{1,0:T(8,128)(2,1)S(1)}, bf16[784,512]{1,0:T(8,128)(2,1)S(1)}, u32[]{:S(2)}, u32[]{:S(2)}) collective-permute-start(bf16[784,512]{1,0:T(8,128)(2,1)S(1)} %get-tuple-element.134), channel_id=1, source_target_pairs={{0,1},{1,0},{2,3},{3,2},{4,5},{5,4},{6,7},{7,6},{8,9},{9,8},{10,11... | collective-permute-start | bytes 2408456 | tf_op jit(solution)/shard_map/ppermute | solution.py:775
  72.6 22.8 %collective-permute-start.15 = (bf16[1,192,512]{2,1,0:T(8,128)(2,1)S(1)}, bf16[1,192,512]{2,1,0:T(8,128)(2,1)S(1)}, u32[]{:S(2)}, u32[]{:S(2)}) collective-permute-start(bf16[1,192,512]{2,1,0:T(8,128)(2,1)S(1)} %get-tuple-element.220), channel_id=1, source_target_pairs={{9,0},{25,1},{11,2},{27,3},{13,4},{29,5},{15,6},{31,7},{1,8},{17,9... | collective-permute-start | bytes 589832 | tf_op jit(solution)/shard_map/ppermute | solution.py:991
  73.6 21.8 %collective-permute-start.16 = (bf16[1,192,512]{2,1,0:T(8,128)(2,1)S(1)}, bf16[1,192,512]{2,1,0:T(8,128)(2,1)S(1)}, u32[]{:S(2)}, u32[]{:S(2)}) collective-permute-start(bf16[1,192,512]{2,1,0:T(8,128)(2,1)S(1)} %get-tuple-element.223), channel_id=1, source_target_pairs={{8,0},{24,1},{10,2},{26,3},{12,4},{28,5},{14,6},{30,7},{0,8},{16,9... | collective-permute-start | bytes 589832 | tf_op jit(solution)/shard_map/ppermute | solution.py:991
  74.5 20.9 %collective-permute-start.17 = (bf16[2,192,512]{2,1,0:T(8,128)(2,1)S(1)}, bf16[2,192,512]{2,1,0:T(8,128)(2,1)S(1)}, u32[]{:S(2)}, u32[]{:S(2)}) collective-permute-start(bf16[2,192,512]{2,1,0:T(8,128)(2,1)S(1)} %pad_maximum_fusion.4), channel_id=1, source_target_pairs={{1,0},{17,1},{3,2},{19,3},{5,4},{21,5},{7,6},{23,7},{9,8},{25,9},{... | collective-permute-start | bytes 1179656 | tf_op jit(solution)/shard_map/ppermute | solution.py:991
  76.1 19.3 %collective-permute-start.18 = (bf16[2,192,512]{2,1,0:T(8,128)(2,1)S(1)}, bf16[2,192,512]{2,1,0:T(8,128)(2,1)S(1)}, u32[]{:S(2)}, u32[]{:S(2)}) collective-permute-start(bf16[2,192,512]{2,1,0:T(8,128)(2,1)S(1)} %pad_maximum_fusion.5), channel_id=1, source_target_pairs={{0,0},{16,1},{2,2},{18,3},{4,4},{20,5},{6,6},{22,7},{8,8},{24,9},{... | collective-permute-start | bytes 1179656 | tf_op jit(solution)/shard_map/ppermute | solution.py:991
  96.4 17.2 %collective-permute-start.20 = (bf16[208,512]{1,0:T(8,128)(2,1)S(1)}, bf16[208,512]{1,0:T(8,128)(2,1)S(1)}, u32[]{:S(2)}, u32[]{:S(2)}) collective-permute-start(bf16[208,512]{1,0:T(8,128)(2,1)S(1)} %get-tuple-element.254), channel_id=1, source_target_pairs={{0,8},{8,0},{16,24},{24,16},{1,9},{9,1},{17,25},{25,17},{2,10},{10... | collective-permute-start | bytes 638984 | tf_op jit(solution)/shard_map/ppermute | solution.py:775
  98.1 15.6 %collective-permute-start.21 = (bf16[208,512]{1,0:T(8,128)(2,1)S(1)}, bf16[208,512]{1,0:T(8,128)(2,1)S(1)}, u32[]{:S(2)}, u32[]{:S(2)}) collective-permute-start(bf16[208,512]{1,0:T(8,128)(2,1)S(1)} %get-tuple-element.256), channel_id=1, source_target_pairs={{0,16},{8,24},{16,0},{24,8},{1,17},{9,25},{17,1},{25,9},{2,18},{10... | collective-permute-start | bytes 638984 | tf_op jit(solution)/shard_map/ppermute | solution.py:775
  99.5 14.1 %collective-permute-start.22 = (bf16[208,512]{1,0:T(8,128)(2,1)S(1)}, bf16[208,512]{1,0:T(8,128)(2,1)S(1)}, u32[]{:S(2)}, u32[]{:S(2)}) collective-permute-start(bf16[208,512]{1,0:T(8,128)(2,1)S(1)} %get-tuple-element.255), channel_id=1, source_target_pairs={{0,24},{8,16},{16,8},{24,0},{1,25},{9,17},{17,9},{25,1},{2,26},{10... | collective-permute-start | bytes 638984 | tf_op jit(solution)/shard_map/ppermute | solution.py:775
  120.1 11.8 %collective-permute-start.25 = (bf16[208,512]{1,0:T(8,128)(2,1)S(1)}, bf16[208,512]{1,0:T(8,128)(2,1)S(1)}, u32[]{:S(2)}, u32[]{:S(2)}) collective-permute-start(bf16[208,512]{1,0:T(8,128)(2,1)S(1)} %get-tuple-element.253), channel_id=1, source_target_pairs={{0,16},{8,24},{16,0},{24,8},{1,17},{9,25},{17,1},{25,9},{2,18},{10... | collective-permute-start | bytes 638984 | tf_op jit(solution)/shard_map/ppermute | solution.py:775
  121.2 10.7 %collective-permute-start.26 = (bf16[208,512]{1,0:T(8,128)(2,1)S(1)}, bf16[208,512]{1,0:T(8,128)(2,1)S(1)}, u32[]{:S(2)}, u32[]{:S(2)}) collective-permute-start(bf16[208,512]{1,0:T(8,128)(2,1)S(1)} %get-tuple-element.252), channel_id=1, source_target_pairs={{0,24},{8,16},{16,8},{24,0},{1,25},{9,17},{17,9},{25,1},{2,26},{10... | collective-permute-start | bytes 638984 | tf_op jit(solution)/shard_map/ppermute | solution.py:775
  132.1 16.2 %collective-permute-start.33 = (bf16[768,512]{1,0:T(8,128)(2,1)S(1)}, bf16[768,512]{1,0:T(8,128)(2,1)S(1)}, u32[]{:S(2)}, u32[]{:S(2)}) collective-permute-start(bf16[768,512]{1,0:T(8,128)(2,1)S(1)} %get-tuple-element.163), channel_id=1, source_target_pairs={{0,1},{1,0},{2,3},{3,2},{4,5},{5,4},{6,7},{7,6},{8,9},{9,8},{10,11... | collective-permute-start | bytes 2359304 | tf_op jit(solution)/shard_map/ppermute | solution.py:775
  132.3 10.0 %collective-permute-start.27 = (bf16[112,512]{1,0:T(8,128)(2,1)S(1)}, bf16[112,512]{1,0:T(8,128)(2,1)S(1)}, u32[]{:S(2)}, u32[]{:S(2)}) collective-permute-start(bf16[112,512]{1,0:T(8,128)(2,1)S(1)} %get-tuple-element.250), channel_id=1, source_target_pairs={{0,2},{1,3},{2,0},{3,1},{4,6},{5,7},{6,4},{7,5},{8,10},{9,11},{10,... | collective-permute-start | bytes 344072 | tf_op jit(solution)/shard_map/ppermute | solution.py:775
  133.9 11.8 %collective-permute-start.28 = (bf16[112,512]{1,0:T(8,128)(2,1)S(1)}, bf16[112,512]{1,0:T(8,128)(2,1)S(1)}, u32[]{:S(2)}, u32[]{:S(2)}) collective-permute-start(bf16[112,512]{1,0:T(8,128)(2,1)S(1)} %get-tuple-element.249), channel_id=1, source_target_pairs={{0,4},{1,5},{2,6},{3,7},{4,0},{5,1},{6,2},{7,3},{8,12},{9,13},{10,... | collective-permute-start | bytes 344072 | tf_op jit(solution)/shard_map/ppermute | solution.py:775
  149.1 19.8 %collective-permute-start.38 = (bf16[2,192,512]{2,1,0:T(8,128)(2,1)S(1)}, bf16[2,192,512]{2,1,0:T(8,128)(2,1)S(1)}, u32[]{:S(2)}, u32[]{:S(2)}) collective-permute-start(bf16[2,192,512]{2,1,0:T(8,128)(2,1)S(1)} %pad_maximum_fusion.10), channel_id=1, source_target_pairs={{9,0},{25,1},{11,2},{27,3},{13,4},{29,5},{15,6},{31,7},{1,8},{17,9... | collective-permute-start | bytes 1179656 | tf_op jit(solution)/shard_map/ppermute | solution.py:1025
  150.3 18.7 %collective-permute-start.37 = (bf16[2,192,512]{2,1,0:T(8,128)(2,1)S(1)}, bf16[2,192,512]{2,1,0:T(8,128)(2,1)S(1)}, u32[]{:S(2)}, u32[]{:S(2)}) collective-permute-start(bf16[2,192,512]{2,1,0:T(8,128)(2,1)S(1)} %pad_maximum_fusion.9), channel_id=1, source_target_pairs={{8,0},{24,1},{10,2},{26,3},{12,4},{28,5},{14,6},{30,7},{0,8},{16,9... | collective-permute-start | bytes 1179656 | tf_op jit(solution)/shard_map/ppermute | solution.py:1025
  151.6 17.4 %collective-permute-start.36 = (bf16[2,192,512]{2,1,0:T(8,128)(2,1)S(1)}, bf16[2,192,512]{2,1,0:T(8,128)(2,1)S(1)}, u32[]{:S(2)}, u32[]{:S(2)}) collective-permute-start(bf16[2,192,512]{2,1,0:T(8,128)(2,1)S(1)} %pad_maximum_fusion.8), channel_id=1, source_target_pairs={{1,0},{17,1},{3,2},{19,3},{5,4},{21,5},{7,6},{23,7},{9,8},{25,9},{... | collective-permute-start | bytes 1179656 | tf_op jit(solution)/shard_map/ppermute | solution.py:1025
  152.5 16.5 %collective-permute-start.35 = (bf16[2,192,512]{2,1,0:T(8,128)(2,1)S(1)}, bf16[2,192,512]{2,1,0:T(8,128)(2,1)}, u32[]{:S(2)}, u32[]{:S(2)}) collective-permute-start(bf16[2,192,512]{2,1,0:T(8,128)(2,1)S(1)} %pad_maximum_fusion.7), channel_id=1, source_target_pairs={{0,0},{16,1},{2,2},{18,3},{4,4},{20,5},{6,6},{22,7},{8,8},{24,9},{... | collective-permute-start | bytes 1179656 | tf_op jit(solution)/shard_map/ppermute | solution.py:1025
  169.1 13.5 %collective-permute-start.39 = (bf16[2,192,512]{2,1,0:T(8,128)(2,1)S(1)}, bf16[2,192,512]{2,1,0:T(8,128)(2,1)S(1)}, u32[]{:S(2)}, u32[]{:S(2)}) collective-permute-start(bf16[2,192,512]{2,1,0:T(8,128)(2,1)S(1)} %pad_maximum_fusion.11), channel_id=1, source_target_pairs={{0,24},{8,16},{16,8},{24,0},{1,25},{9,17},{17,9},{25,1},{2,26},{10... | collective-permute-start | bytes 1179656 | tf_op jit(solution)/shard_map/ppermute | solution.py:775
  172.5 17.4 %collective-permute-start.40 = (bf16[2,192,512]{2,1,0:T(8,128)(2,1)S(1)}, bf16[2,192,512]{2,1,0:T(8,128)(2,1)S(1)}, u32[]{:S(2)}, u32[]{:S(2)}) collective-permute-start(bf16[2,192,512]{2,1,0:T(8,128)(2,1)S(1)} %pad_maximum_fusion.11), channel_id=1, source_target_pairs={{0,16},{8,24},{16,0},{24,8},{1,17},{9,25},{17,1},{25,9},{2,18},{10... | collective-permute-start | bytes 1179656 | tf_op jit(solution)/shard_map/ppermute | solution.py:775
  172.5 17.4 %collective-permute-start.41 = (bf16[2,192,512]{2,1,0:T(8,128)(2,1)S(1)}, bf16[2,192,512]{2,1,0:T(8,128)(2,1)S(1)}, u32[]{:S(2)}, u32[]{:S(2)}) collective-permute-start(bf16[2,192,512]{2,1,0:T(8,128)(2,1)S(1)} %pad_maximum_fusion.11), channel_id=1, source_target_pairs={{0,8},{8,0},{16,24},{24,16},{1,9},{9,1},{17,25},{25,17},{2,10},{10... | collective-permute-start | bytes 1179656 | tf_op jit(solution)/shard_map/ppermute | solution.py:775
  (67 other events, 541.9 us)
